TPU v7x, 512 devices: a whole 4x4x16 slice. The times are simulated.
512 devices in a mesh: dp: 64 (over x, y, z_lo), section: 8 (over z_hi, core).
Axes of the slice: x: 4, y: 4, z: 16 (z_hi: 4, z_lo: 4; z = z_hi * 4 + z_lo), core: 2. Of those that a mesh axis runs over, the one named last changes fastest.
Arguments:
- latents: bfloat16 [64, 4, 8, 8, 256], P('dp'), may hold values from -6 to 6
- cotangent: bfloat16 [64, 4, 8, 8, 256], P('dp'), may hold values from -0.046875 to 0.046875
- spatial_weight: bfloat16 [8, 2304, 256], P('section'), may hold values from -0.125 to 0.125
- temporal_weight: bfloat16 [8, 768, 256], P('section'), may hold values from -0.21875 to 0.21875
- norm_gain: float32 [8, 256], P('section'), may hold values from 0.25 to 1.75
- norm_shift: float32 [8, 256], P('section'), may hold values from -3 to 3
Outputs:
- spatial_grad: float32 [8, 2304, 256], P('section', 'dp')
- temporal_grad: float32 [8, 768, 256], P('section', 'dp')
- norm_grad: float32 [8, 2, 256], P('section')
All inputs are finite; a program needn't handle non-finite values.
Results may differ from a plain program's by a relative error of at most 0.015.
Values may be sent and summed in bfloat16 or wider, within the bound.
A program may use at most 64 MiB of HBM per device.

v0:
```python
import jax
import jax.numpy as jnp
from jax import lax
from jax.sharding import PartitionSpec as P

GROUPS = 32


epsilon = 1e-05
spatial_offsets = (
    (0, -1, -1),
    (0, -1, 0),
    (0, -1, 1),
    (0, 0, -1),
    (0, 0, 0),
    (0, 0, 1),
    (0, 1, -1),
    (0, 1, 0),
    (0, 1, 1),
)
temporal_offsets = ((-1, 0, 0), (0, 0, 0), (1, 0, 0))


def swapped(value, axis, bit):
    mask = 2**bit
    pairs = [(source, source ^ mask) for source in range(lax.axis_size(axis))]
    return lax.ppermute(value, axis, pairs)


def from_behind(shard, axis, by):
    devices = lax.axis_size(axis)
    pairs = [(i, i + by) for i in range(devices) if 0 <= i + by < devices]
    return lax.ppermute(shard, axis, pairs)


def shifted(field, offset):
    frames, height, columns, channels = field.shape
    padded = jnp.pad(field, ((1, 1), (1, 1), (1, 1), (0, 0)))
    return padded[
        1 + offset[0] : 1 + offset[0] + frames,
        1 + offset[1] : 1 + offset[1] + height,
        1 + offset[2] : 1 + offset[2] + columns,
        :,
    ]


def stacked(field, offsets, sign):
    parts = [
        shifted(field, (sign * offset[0], sign * offset[1], sign * offset[2])) for offset in offsets
    ]
    joined = jnp.concatenate(parts, axis=3)
    return joined.reshape(-1, joined.shape[3])


def contract_rows(left, right):
    return lax.dot_general(
        left, right, (((0,), (0,)), ((), ())), preferred_element_type=jnp.float32
    )


def apply_back(columns_in, weight, taps):
    rows = columns_in.shape[0]
    channels = weight.shape[1]
    return lax.dot_general(
        columns_in.reshape(rows, taps, channels),
        weight.reshape(taps, channels, channels),
        (((1, 2), (0, 2)), ((), ())),
        preferred_element_type=jnp.float32,
    )


def section_parts(inputs, spatial, temporal, gain, shift):
    frames, height, columns, channels = inputs.shape
    rows = frames * height * columns
    grouped = inputs.reshape(rows, GROUPS, channels // GROUPS)
    center = jnp.mean(grouped, axis=(0, 2), keepdims=True)
    deviation = grouped - center
    variance = jnp.mean(deviation * deviation, axis=(0, 2), keepdims=True)
    scaling = lax.rsqrt(variance + epsilon)
    normed = (deviation * scaling).reshape(rows, channels)
    before = normed * gain + shift
    active = (before * jax.nn.sigmoid(before)).astype(jnp.bfloat16).reshape(inputs.shape)
    middle = (
        jnp.dot(stacked(active, spatial_offsets, 1), spatial, preferred_element_type=jnp.float32)
        .astype(jnp.bfloat16)
        .reshape(inputs.shape)
    )
    branch = jnp.dot(
        stacked(middle, temporal_offsets, 1), temporal, preferred_element_type=jnp.float32
    )
    output = (inputs.reshape(rows, channels) + branch).astype(jnp.bfloat16).reshape(inputs.shape)
    return (output, normed, before, active, middle, scaling)


def section_backward(inputs, upstream, spatial, temporal, gain, shift):
    output, normed, before, active, middle, scaling = section_parts(
        inputs, spatial, temporal, gain, shift
    )
    rows, channels = normed.shape
    flat_up = upstream.reshape(rows, channels)
    temporal_term = contract_rows(stacked(middle, temporal_offsets, 1), flat_up)
    middle_grad = (
        apply_back(stacked(upstream, temporal_offsets, -1), temporal, 3)
        .astype(jnp.bfloat16)
        .reshape(upstream.shape)
    )
    spatial_term = contract_rows(
        stacked(active, spatial_offsets, 1), middle_grad.reshape(rows, channels)
    )
    active_grad = apply_back(stacked(middle_grad, spatial_offsets, -1), spatial, 9)
    sigma = jax.nn.sigmoid(before)
    before_grad = active_grad * sigma * (1.0 + before * (1.0 - sigma))
    gain_term = jnp.sum(before_grad * normed, axis=0)
    shift_term = jnp.sum(before_grad, axis=0)
    normed_grad = (before_grad * gain).reshape(rows, GROUPS, channels // GROUPS)
    grouped_normed = normed.reshape(rows, GROUPS, channels // GROUPS)
    inner = jnp.mean(normed_grad, axis=(0, 2), keepdims=True)
    project = jnp.mean(normed_grad * grouped_normed, axis=(0, 2), keepdims=True)
    input_grad = scaling * (normed_grad - inner - grouped_normed * project)
    total = (
        (flat_up.astype(jnp.float32) + input_grad.reshape(rows, channels))
        .astype(jnp.bfloat16)
        .reshape(upstream.shape)
    )
    return (total, spatial_term, temporal_term, gain_term, shift_term)


def shards(latents, cotangent, spatial_weight, temporal_weight, norm_gain, norm_shift):
    sections = lax.axis_size("section")
    position = lax.axis_index("section")
    midpoint = sections // 2
    batches = latents.shape[0]
    decoder = position >= midpoint
    mirror = sections - 1 - position
    bit_count = sections.bit_length() - 1
    spatial = spatial_weight[0]
    temporal = temporal_weight[0]
    gain = norm_gain[0]
    shift = norm_shift[0]
    field_shape = latents.shape[1:]
    blank = jnp.zeros(field_shape, jnp.bfloat16)

    def mirrored(field):
        for bit_index in range(bit_count):
            field = swapped(field, "section", bit_index)
        return field

    def forward_tick(tick, carry):
        incoming, skip_store, saved = carry
        micro = tick - position
        active = (micro >= 0) & (micro < batches)
        index_slot = jnp.clip(micro, 0, batches - 1)
        first = lax.dynamic_index_in_dim(latents, index_slot, 0, keepdims=False)
        arriving = jnp.where(position == 0, first, incoming)
        skip_in = jnp.where(
            decoder, lax.dynamic_index_in_dim(skip_store, index_slot, 0, keepdims=False), blank
        )
        inputs = arriving.astype(jnp.float32) + skip_in.astype(jnp.float32)
        output = lax.cond(
            active,
            lambda value: section_parts(value, spatial, temporal, gain, shift)[0],
            lambda value: blank,
            inputs,
        )
        saved = jnp.where(
            active, lax.dynamic_update_index_in_dim(saved, inputs, index_slot, 0), saved
        )
        passed = from_behind(output, "section", 1)
        received = mirrored(output)
        source = tick - mirror
        wanted = decoder & (source >= 0) & (source < batches)
        store_slot = jnp.clip(source, 0, batches - 1)
        skip_store = jnp.where(
            wanted, lax.dynamic_update_index_in_dim(skip_store, received, store_slot, 0), skip_store
        )
        return (passed, skip_store, saved)

    tick_count = batches + sections - 1
    start = (blank, jnp.zeros(latents.shape, jnp.bfloat16), jnp.zeros(latents.shape, jnp.float32))
    unused_field, unused_store, saved = lax.fori_loop(0, tick_count, forward_tick, start)
    empty_result = (
        blank,
        jnp.zeros(spatial.shape, jnp.float32),
        jnp.zeros(temporal.shape, jnp.float32),
        jnp.zeros(gain.shape, jnp.float32),
        jnp.zeros(shift.shape, jnp.float32),
    )

    def backward_tick(tick, carry):
        incoming, grad_store, acc_spatial, acc_temporal, acc_gain, acc_shift = carry
        micro = tick - mirror
        active = (micro >= 0) & (micro < batches)
        index_slot = jnp.clip(micro, 0, batches - 1)
        last_cot = lax.dynamic_index_in_dim(cotangent, index_slot, 0, keepdims=False)
        base = jnp.where(position == sections - 1, last_cot, incoming)
        extra = jnp.where(
            decoder, blank, lax.dynamic_index_in_dim(grad_store, index_slot, 0, keepdims=False)
        )
        upstream = (base.astype(jnp.float32) + extra.astype(jnp.float32)).astype(jnp.bfloat16)
        inputs = lax.dynamic_index_in_dim(saved, index_slot, 0, keepdims=False)
        result = lax.cond(
            active,
            lambda pair: section_backward(pair[0], pair[1], spatial, temporal, gain, shift),
            lambda pair: empty_result,
            (inputs, upstream),
        )
        returning = result[0]
        acc_spatial = acc_spatial + result[1]
        acc_temporal = acc_temporal + result[2]
        acc_gain = acc_gain + result[3]
        acc_shift = acc_shift + result[4]
        passed = from_behind(returning, "section", -1)
        received = mirrored(returning)
        source = tick - position
        wanted = jnp.logical_not(decoder) & (source >= 0) & (source < batches)
        store_slot = jnp.clip(source, 0, batches - 1)
        grad_store = jnp.where(
            wanted, lax.dynamic_update_index_in_dim(grad_store, received, store_slot, 0), grad_store
        )
        return (passed, grad_store, acc_spatial, acc_temporal, acc_gain, acc_shift)

    begin = (
        blank,
        jnp.zeros(latents.shape, jnp.bfloat16),
        empty_result[1],
        empty_result[2],
        empty_result[3],
        empty_result[4],
    )
    finished = lax.fori_loop(0, tick_count, backward_tick, begin)
    spatial_sum, temporal_sum = (
        lax.psum_scatter(finished[2], "dp", scatter_dimension=0, tiled=True),
        lax.psum_scatter(finished[3], "dp", scatter_dimension=0, tiled=True),
    )
    norm_total = lax.psum(jnp.stack([finished[4], finished[5]]), "dp")
    return (spatial_sum[None], temporal_sum[None], norm_total[None])


def solution(mesh):
    return jax.shard_map(
        shards,
        mesh=mesh,
        in_specs=(
            P("dp", None, None, None, None),
            P("dp", None, None, None, None),
            P("section", None, None),
            P("section", None, None),
            P("section", None),
            P("section", None),
        ),
        out_specs=(P("section", "dp", None), P("section", "dp", None), P("section", None, None)),
        check_vma=False,
    )
```

profile of v0, /device:TPU:6, one launch (start us, length us, event | category | flops | bytes accessed | tf_op | source)
XLA Modules:
  0.0 1272.0 jit_solution(14043021675467633781)
XLA Ops:
  0.7 350.6 %while.44 = (s32[]{:T(128)}, bf16[4,8,8,256]{3,2,1,0:T(8,128)(2,1)S(1)}, bf16[1,4,8,8,256]{4,3,2,1,0:T(8,128)(2,1)S(1)}, f32[1,4,8,8,256]{4,3,2,1,0:T(8,128)S(1)...) while((s32[]{:T(128)}, ...), condition=%wide.region_7.8_spmd.clone, body=%wide.region_0.7_spmd.clone.sunk | while | flops 405536800 | bytes 18510388 | solution.py:180
  14.4 13.2 %collective-permute-done.2 = bf16[4,8,8,256]{3,2,1,0:T(8,128)(2,1)S(1)} collective-permute-done((bf16[4,8,8,256]{3,2,1,0:T(8,128)(2,1)S(1)}, bf16[4,8,8,256]{3,2,1,0:T(8,128)(2,1)S(1)}, u32[]{:S(2)}, u32[]{:S(2)}) %collective-permute-start.2) | collective-permute-done | bytes 131104 | tf_op jit(solution)/shard_map/while/body/eval_jaxpr/ppermute | solution.py:27
  27.7 13.2 %collective-permute-start.3 = (bf16[4,8,8,256]{3,2,1,0:T(8,128)(2,1)S(1)}, bf16[4,8,8,256]{3,2,1,0:T(8,128)(2,1)S(1)}, u32[]{:S(2)}, u32[]{:S(2)}) collective-permute-start(bf16[4,8,8,256]{3,2,1,0:T(8,128)(2,1)S(1)} %collective-permute-done.2), channel_id=1, source_target_pairs={{0,4},{1,5},{2,6},{3,7},{4,0},{5,1},{6,2},{7,3},{8,12},{9,13},{10,... | collective-permute-start | bytes 393224 | tf_op jit(solution)/shard_map/while/body/eval_jaxpr/ppermute | solution.py:27
  42.2 8.5 collective-permute-done.3
  60.5 14.6 %collective-permute-done.2 = bf16[4,8,8,256]{3,2,1,0:T(8,128)(2,1)S(1)} collective-permute-done((bf16[4,8,8,256]{3,2,1,0:T(8,128)(2,1)S(1)}, bf16[4,8,8,256]{3,2,1,0:T(8,128)(2,1)S(1)}, u32[]{:S(2)}, u32[]{:S(2)}) %collective-permute-start.2) | collective-permute-done | bytes 131104 | tf_op jit(solution)/shard_map/while/body/eval_jaxpr/ppermute | solution.py:27
  75.1 9.9 collective-permute-start.3
  86.3 16.4 %collective-permute-done.3 = bf16[4,8,8,256]{3,2,1,0:T(8,128)(2,1)S(1)} collective-permute-done((bf16[4,8,8,256]{3,2,1,0:T(8,128)(2,1)S(1)}, bf16[4,8,8,256]{3,2,1,0:T(8,128)(2,1)S(1)}, u32[]{:S(2)}, u32[]{:S(2)}) %collective-permute-start.3) | collective-permute-done | bytes 131104 | tf_op jit(solution)/shard_map/while/body/eval_jaxpr/ppermute | solution.py:27
  109.3 12.7 %collective-permute-done.2 = bf16[4,8,8,256]{3,2,1,0:T(8,128)(2,1)S(1)} collective-permute-done((bf16[4,8,8,256]{3,2,1,0:T(8,128)(2,1)S(1)}, bf16[4,8,8,256]{3,2,1,0:T(8,128)(2,1)S(1)}, u32[]{:S(2)}, u32[]{:S(2)}) %collective-permute-start.2) | collective-permute-done | bytes 131104 | tf_op jit(solution)/shard_map/while/body/eval_jaxpr/ppermute | solution.py:27
  129.4 17.2 %collective-permute-done.3 = bf16[4,8,8,256]{3,2,1,0:T(8,128)(2,1)S(1)} collective-permute-done((bf16[4,8,8,256]{3,2,1,0:T(8,128)(2,1)S(1)}, bf16[4,8,8,256]{3,2,1,0:T(8,128)(2,1)S(1)}, u32[]{:S(2)}, u32[]{:S(2)}) %collective-permute-start.3) | collective-permute-done | bytes 131104 | tf_op jit(solution)/shard_map/while/body/eval_jaxpr/ppermute | solution.py:27
  153.5 10.7 collective-permute-done.2
  173.2 14.5 %collective-permute-done.3 = bf16[4,8,8,256]{3,2,1,0:T(8,128)(2,1)S(1)} collective-permute-done((bf16[4,8,8,256]{3,2,1,0:T(8,128)(2,1)S(1)}, bf16[4,8,8,256]{3,2,1,0:T(8,128)(2,1)S(1)}, u32[]{:S(2)}, u32[]{:S(2)}) %collective-permute-start.3) | collective-permute-done | bytes 131104 | tf_op jit(solution)/shard_map/while/body/eval_jaxpr/ppermute | solution.py:27
  195.6 16.6 %collective-permute-done.2 = bf16[4,8,8,256]{3,2,1,0:T(8,128)(2,1)S(1)} collective-permute-done((bf16[4,8,8,256]{3,2,1,0:T(8,128)(2,1)S(1)}, bf16[4,8,8,256]{3,2,1,0:T(8,128)(2,1)S(1)}, u32[]{:S(2)}, u32[]{:S(2)}) %collective-permute-start.2) | collective-permute-done | bytes 131104 | tf_op jit(solution)/shard_map/while/body/eval_jaxpr/ppermute | solution.py:27
  217.1 15.4 %collective-permute-done.3 = bf16[4,8,8,256]{3,2,1,0:T(8,128)(2,1)S(1)} collective-permute-done((bf16[4,8,8,256]{3,2,1,0:T(8,128)(2,1)S(1)}, bf16[4,8,8,256]{3,2,1,0:T(8,128)(2,1)S(1)}, u32[]{:S(2)}, u32[]{:S(2)}) %collective-permute-start.3) | collective-permute-done | bytes 131104 | tf_op jit(solution)/shard_map/while/body/eval_jaxpr/ppermute | solution.py:27
  239.2 11.6 collective-permute-done.2
  250.8 8.4 collective-permute-start.3
  260.8 9.2 collective-permute-done.3
  278.5 16.0 %collective-permute-done.2 = bf16[4,8,8,256]{3,2,1,0:T(8,128)(2,1)S(1)} collective-permute-done((bf16[4,8,8,256]{3,2,1,0:T(8,128)(2,1)S(1)}, bf16[4,8,8,256]{3,2,1,0:T(8,128)(2,1)S(1)}, u32[]{:S(2)}, u32[]{:S(2)}) %collective-permute-start.2) | collective-permute-done | bytes 131104 | tf_op jit(solution)/shard_map/while/body/eval_jaxpr/ppermute | solution.py:27
  303.6 9.0 collective-permute-done.3
  320.6 12.1 collective-permute-done.2
  340.4 10.9 collective-permute-done.3
  352.0 405.7 %while.45 = (s32[]{:T(128)}, bf16[4,8,8,256]{3,2,1,0:T(8,128)(2,1)}, bf16[1,4,8,8,256]{4,3,2,1,0:T(8,128)(2,1)S(1)}, f32[2304,256]{1,0:T(8,128)}, f32[768,256]{1...) while((s32[]{:T(128)}, ...), condition=%wide.region_21.22_spmd.clone, body=%wide.region_8.21_spmd.clone.sunk | while | flops 1115030016 | bytes 55383960 | solution.py:230
  360.1 8.6 collective-permute-start.6
  372.4 13.3 %collective-permute-start.7 = (bf16[4,8,8,256]{3,2,1,0:T(8,128)(2,1)S(1)}, bf16[4,8,8,256]{3,2,1,0:T(8,128)(2,1)S(1)}, u32[]{:S(2)}, u32[]{:S(2)}) collective-permute-start(bf16[4,8,8,256]{3,2,1,0:T(8,128)(2,1)S(1)} %collective-permute-done.6), channel_id=1, source_target_pairs={{0,4},{1,5},{2,6},{3,7},{4,0},{5,1},{6,2},{7,3},{8,12},{9,13},{10,... | collective-permute-start | bytes 393224 | tf_op jit(solution)/shard_map/while/body/eval_jaxpr/ppermute | solution.py:27
  386.4 8.4 collective-permute-done.7
  404.8 8.5 collective-permute-start.6
  418.8 21.4 %collective-permute-start.7 = (bf16[4,8,8,256]{3,2,1,0:T(8,128)(2,1)S(1)}, bf16[4,8,8,256]{3,2,1,0:T(8,128)(2,1)S(1)}, u32[]{:S(2)}, u32[]{:S(2)}) collective-permute-start(bf16[4,8,8,256]{3,2,1,0:T(8,128)(2,1)S(1)} %collective-permute-done.6), channel_id=1, source_target_pairs={{0,4},{1,5},{2,6},{3,7},{4,0},{5,1},{6,2},{7,3},{8,12},{9,13},{10,... | collective-permute-start | bytes 393224 | tf_op jit(solution)/shard_map/while/body/eval_jaxpr/ppermute | solution.py:27
  458.4 8.5 collective-permute-start.6
  472.3 20.4 %collective-permute-start.7 = (bf16[4,8,8,256]{3,2,1,0:T(8,128)(2,1)S(1)}, bf16[4,8,8,256]{3,2,1,0:T(8,128)(2,1)S(1)}, u32[]{:S(2)}, u32[]{:S(2)}) collective-permute-start(bf16[4,8,8,256]{3,2,1,0:T(8,128)(2,1)S(1)} %collective-permute-done.6), channel_id=1, source_target_pairs={{0,4},{1,5},{2,6},{3,7},{4,0},{5,1},{6,2},{7,3},{8,12},{9,13},{10,... | collective-permute-start | bytes 393224 | tf_op jit(solution)/shard_map/while/body/eval_jaxpr/ppermute | solution.py:27
  508.8 8.6 collective-permute-start.6
  523.8 22.0 %collective-permute-start.7 = (bf16[4,8,8,256]{3,2,1,0:T(8,128)(2,1)S(1)}, bf16[4,8,8,256]{3,2,1,0:T(8,128)(2,1)S(1)}, u32[]{:S(2)}, u32[]{:S(2)}) collective-permute-start(bf16[4,8,8,256]{3,2,1,0:T(8,128)(2,1)S(1)} %collective-permute-done.6), channel_id=1, source_target_pairs={{0,4},{1,5},{2,6},{3,7},{4,0},{5,1},{6,2},{7,3},{8,12},{9,13},{10,... | collective-permute-start | bytes 393224 | tf_op jit(solution)/shard_map/while/body/eval_jaxpr/ppermute | solution.py:27
  560.8 9.7 collective-permute-start.6
  575.3 14.2 %collective-permute-start.7 = (bf16[4,8,8,256]{3,2,1,0:T(8,128)(2,1)S(1)}, bf16[4,8,8,256]{3,2,1,0:T(8,128)(2,1)S(1)}, u32[]{:S(2)}, u32[]{:S(2)}) collective-permute-start(bf16[4,8,8,256]{3,2,1,0:T(8,128)(2,1)S(1)} %collective-permute-done.6), channel_id=1, source_target_pairs={{0,4},{1,5},{2,6},{3,7},{4,0},{5,1},{6,2},{7,3},{8,12},{9,13},{10,... | collective-permute-start | bytes 393224 | tf_op jit(solution)/shard_map/while/body/eval_jaxpr/ppermute | solution.py:27
  603.5 23.3 %collective-permute-start.6 = (bf16[4,8,8,256]{3,2,1,0:T(8,128)(2,1)S(1)}, bf16[4,8,8,256]{3,2,1,0:T(8,128)(2,1)S(1)}, u32[]{:S(2)}, u32[]{:S(2)}) collective-permute-start(bf16[4,8,8,256]{3,2,1,0:T(8,128)(2,1)S(1)} %collective-permute-done.5), channel_id=1, source_target_pairs={{0,2},{1,3},{2,0},{3,1},{4,6},{5,7},{6,4},{7,5},{8,10},{9,11},{10,... | collective-permute-start | bytes 393224 | tf_op jit(solution)/shard_map/while/body/eval_jaxpr/ppermute | solution.py:27
  635.8 9.9 collective-permute-start.7
  646.4 8.1 collective-permute-done.7
  657.7 13.3 %collective-permute-start.5 = (bf16[4,8,8,256]{3,2,1,0:T(8,128)(2,1)}, bf16[4,8,8,256]{3,2,1,0:T(8,128)(2,1)S(1)}, u32[]{:S(2)}, u32[]{:S(2)}) collective-permute-start(bf16[4,8,8,256]{3,2,1,0:T(8,128)(2,1)} %get-tuple-element.1080), channel_id=1, source_target_pairs={{0,1},{1,0},{2,3},{3,2},{4,5},{5,4},{6,7},{7,6},{8,9},{9,8},{10,11... | collective-permute-start | bytes 393224 | tf_op jit(solution)/shard_map/while/body/eval_jaxpr/ppermute | solution.py:27
  675.8 8.1 collective-permute-start.6
  691.5 14.0 %collective-permute-done.7 = bf16[4,8,8,256]{3,2,1,0:T(8,128)(2,1)S(1)} collective-permute-done((bf16[4,8,8,256]{3,2,1,0:T(8,128)(2,1)S(1)}, bf16[4,8,8,256]{3,2,1,0:T(8,128)(2,1)S(1)}, u32[]{:S(2)}, u32[]{:S(2)}) %collective-permute-start.7) | collective-permute-done | bytes 131104 | tf_op jit(solution)/shard_map/while/body/eval_jaxpr/ppermute | solution.py:27
  706.7 14.6 %conditional.7 = (bf16[4,8,8,256]{3,2,1,0:T(8,128)(2,1)}, f32[2304,256]{1,0:T(8,128)S(1)}, f32[768,256]{1,0:T(8,128)S(1)}, f32[256]{0:T(256)}, f32[256]{0:T(256)}) conditional(s32[]{:T(128)} %convert_element_type.171, () %tuple.125, (bf16[4,8,8,256]{3,2,1,0:T(8,128)(2,1)S(1)}, f32[1,4,8,8,256]{4,3,2,1,0:T(8,128)S(1)}, ...), branch_computations={%region_9.9_spmd, %region_10.20_spmd} | conditional | flops 1112866304 | bytes 35577088 | solution.py:201
  728.1 8.6 collective-permute-start.6
  745.5 12.1 collective-permute-done.7
  757.7 226.2 %fusion.40 = (f32[40,256]{1,0:T(8,128)S(1)}, f32[16,256]{1,0:T(8,128)S(1)}) fusion(f32[2304,256]{1,0:T(8,128)} %get-tuple-element.660, f32[768,256]{1,0:T(8,128)} %get-tuple-element.661), kind=kCustom, calls=%all-reduce-scatter.2 | all-reduce-scatter fusion | flops 917506 | bytes 3205120
  989.1 8.4 collective-permute-start.17
  997.5 13.6 %collective-permute-start.18 = (f32[16,256]{1,0:T(8,128)S(1)}, f32[16,256]{1,0:T(8,128)S(1)}, u32[]{:S(2)}, u32[]{:S(2)}) collective-permute-start(f32[16,256]{1,0:T(8,128)S(1)} %get-tuple-element.845), channel_id=1, source_target_pairs={{0,32},{8,40},{16,48},{24,56},{32,64},{40,72},{48,80},{56,88},{64,... | collective-permute-start | bytes 49160
  1011.2 14.4 %collective-permute-start.19 = (f32[16,256]{1,0:T(8,128)S(1)}, f32[16,256]{1,0:T(8,128)S(1)}, u32[]{:S(2)}, u32[]{:S(2)}) collective-permute-start(f32[16,256]{1,0:T(8,128)S(1)} %get-tuple-element.845), channel_id=1, source_target_pairs={{0,40},{8,48},{16,56},{24,64},{32,72},{40,80},{48,88},{56,96},{64,... | collective-permute-start | bytes 49160
  1054.8 166.1 %psum.7 = f32[1,2,256]{2,1,0:T(2,128)} all-reduce(f32[1,2,256]{2,1,0:T(2,128)S(1)} %maximum_bitcast_fusion), channel_id=1, replica_groups=mesh['dp'=64,'section'=8] {'dp'}, use_global_device_ids=true, to_apply=%region_24.25 | all-reduce | flops 512 | bytes 4096 | tf_op jit(solution)/shard_map/psum | solution.py:235
  1222.9 13.4 %collective-permute-start.12 = (f32[40,256]{1,0:T(8,128)S(1)}, f32[40,256]{1,0:T(8,128)S(1)}, u32[]{:S(2)}, u32[]{:S(2)}) collective-permute-start(f32[40,256]{1,0:T(8,128)S(1)} %get-tuple-element.844), channel_id=1, source_target_pairs={{0,40},{8,48},{16,56},{24,64},{32,72},{40,80},{48,88},{56,96},{64,... | collective-permute-start | bytes 122888
  1236.3 20.5 %collective-permute-start.13 = (f32[40,256]{1,0:T(8,128)S(1)}, f32[40,256]{1,0:T(8,128)S(1)}, u32[]{:S(2)}, u32[]{:S(2)}) collective-permute-start(f32[40,256]{1,0:T(8,128)S(1)} %get-tuple-element.844), channel_id=1, source_target_pairs={{0,48},{8,56},{16,64},{24,72},{32,80},{40,88},{48,96},{56,104},{64... | collective-permute-start | bytes 122888
  (504 shorter events, 340.7 us)
Async XLA Ops:
  7.9 19.8 %collective-permute-start.2 = (bf16[4,8,8,256]{3,2,1,0:T(8,128)(2,1)S(1)}, bf16[4,8,8,256]{3,2,1,0:T(8,128)(2,1)S(1)}, u32[]{:S(2)}, u32[]{:S(2)}) collective-permute-start(bf16[4,8,8,256]{3,2,1,0:T(8,128)(2,1)S(1)} %collective-permute-done.1), channel_id=1, source_target_pairs={{0,2},{1,3},{2,0},{3,1},{4,6},{5,7},{6,4},{7,5},{8,10},{9,11},{10,... | collective-permute-start | bytes 393224 | tf_op jit(solution)/shard_map/while/body/eval_jaxpr/ppermute | solution.py:27
  27.7 23.0 %collective-permute-start.3 = (bf16[4,8,8,256]{3,2,1,0:T(8,128)(2,1)S(1)}, bf16[4,8,8,256]{3,2,1,0:T(8,128)(2,1)S(1)}, u32[]{:S(2)}, u32[]{:S(2)}) collective-permute-start(bf16[4,8,8,256]{3,2,1,0:T(8,128)(2,1)S(1)} %collective-permute-done.2), channel_id=1, source_target_pairs={{0,4},{1,5},{2,6},{3,7},{4,0},{5,1},{6,2},{7,3},{8,12},{9,13},{10,... | collective-permute-start | bytes 393224 | tf_op jit(solution)/shard_map/while/body/eval_jaxpr/ppermute | solution.py:27
  55.3 19.8 %collective-permute-start.2 = (bf16[4,8,8,256]{3,2,1,0:T(8,128)(2,1)S(1)}, bf16[4,8,8,256]{3,2,1,0:T(8,128)(2,1)S(1)}, u32[]{:S(2)}, u32[]{:S(2)}) collective-permute-start(bf16[4,8,8,256]{3,2,1,0:T(8,128)(2,1)S(1)} %collective-permute-done.1), channel_id=1, source_target_pairs={{0,2},{1,3},{2,0},{3,1},{4,6},{5,7},{6,4},{7,5},{8,10},{9,11},{10,... | collective-permute-start | bytes 393224 | tf_op jit(solution)/shard_map/while/body/eval_jaxpr/ppermute | solution.py:27
  75.1 27.6 %collective-permute-start.3 = (bf16[4,8,8,256]{3,2,1,0:T(8,128)(2,1)S(1)}, bf16[4,8,8,256]{3,2,1,0:T(8,128)(2,1)S(1)}, u32[]{:S(2)}, u32[]{:S(2)}) collective-permute-start(bf16[4,8,8,256]{3,2,1,0:T(8,128)(2,1)S(1)} %collective-permute-done.2), channel_id=1, source_target_pairs={{0,4},{1,5},{2,6},{3,7},{4,0},{5,1},{6,2},{7,3},{8,12},{9,13},{10,... | collective-permute-start | bytes 393224 | tf_op jit(solution)/shard_map/while/body/eval_jaxpr/ppermute | solution.py:27
  85.0 17.8 %collective-permute-start = (bf16[4,8,8,256]{3,2,1,0:T(8,128)(2,1)S(1)}, bf16[4,8,8,256]{3,2,1,0:T(8,128)(2,1)S(1)}, u32[]{:S(2)}, u32[]{:S(2)}) collective-permute-start(bf16[4,8,8,256]{3,2,1,0:T(8,128)(2,1)S(1)} %get-tuple-element.1205), channel_id=1, source_target_pairs={{0,1},{1,2},{2,3},{3,4},{4,5},{5,6},{6,7},{8,9},{9,10},{10,11},{11... | collective-permute-start | bytes 393224 | tf_op jit(solution)/shard_map/while/body/eval_jaxpr/ppermute | solution.py:33
  122.0 24.6 %collective-permute-start.3 = (bf16[4,8,8,256]{3,2,1,0:T(8,128)(2,1)S(1)}, bf16[4,8,8,256]{3,2,1,0:T(8,128)(2,1)S(1)}, u32[]{:S(2)}, u32[]{:S(2)}) collective-permute-start(bf16[4,8,8,256]{3,2,1,0:T(8,128)(2,1)S(1)} %collective-permute-done.2), channel_id=1, source_target_pairs={{0,4},{1,5},{2,6},{3,7},{4,0},{5,1},{6,2},{7,3},{8,12},{9,13},{10,... | collective-permute-start | bytes 393224 | tf_op jit(solution)/shard_map/while/body/eval_jaxpr/ppermute | solution.py:27
  127.7 19.0 %collective-permute-start = (bf16[4,8,8,256]{3,2,1,0:T(8,128)(2,1)S(1)}, bf16[4,8,8,256]{3,2,1,0:T(8,128)(2,1)S(1)}, u32[]{:S(2)}, u32[]{:S(2)}) collective-permute-start(bf16[4,8,8,256]{3,2,1,0:T(8,128)(2,1)S(1)} %get-tuple-element.1205), channel_id=1, source_target_pairs={{0,1},{1,2},{2,3},{3,4},{4,5},{5,6},{6,7},{8,9},{9,10},{10,11},{11... | collective-permute-start | bytes 393224 | tf_op jit(solution)/shard_map/while/body/eval_jaxpr/ppermute | solution.py:33
  164.2 23.5 %collective-permute-start.3 = (bf16[4,8,8,256]{3,2,1,0:T(8,128)(2,1)S(1)}, bf16[4,8,8,256]{3,2,1,0:T(8,128)(2,1)S(1)}, u32[]{:S(2)}, u32[]{:S(2)}) collective-permute-start(bf16[4,8,8,256]{3,2,1,0:T(8,128)(2,1)S(1)} %collective-permute-done.2), channel_id=1, source_target_pairs={{0,4},{1,5},{2,6},{3,7},{4,0},{5,1},{6,2},{7,3},{8,12},{9,13},{10,... | collective-permute-start | bytes 393224 | tf_op jit(solution)/shard_map/while/body/eval_jaxpr/ppermute | solution.py:27
  171.8 15.9 %collective-permute-start = (bf16[4,8,8,256]{3,2,1,0:T(8,128)(2,1)S(1)}, bf16[4,8,8,256]{3,2,1,0:T(8,128)(2,1)S(1)}, u32[]{:S(2)}, u32[]{:S(2)}) collective-permute-start(bf16[4,8,8,256]{3,2,1,0:T(8,128)(2,1)S(1)} %get-tuple-element.1205), channel_id=1, source_target_pairs={{0,1},{1,2},{2,3},{3,4},{4,5},{5,6},{6,7},{8,9},{9,10},{10,11},{11... | collective-permute-start | bytes 393224 | tf_op jit(solution)/shard_map/while/body/eval_jaxpr/ppermute | solution.py:33
  192.4 19.8 %collective-permute-start.2 = (bf16[4,8,8,256]{3,2,1,0:T(8,128)(2,1)S(1)}, bf16[4,8,8,256]{3,2,1,0:T(8,128)(2,1)S(1)}, u32[]{:S(2)}, u32[]{:S(2)}) collective-permute-start(bf16[4,8,8,256]{3,2,1,0:T(8,128)(2,1)S(1)} %collective-permute-done.1), channel_id=1, source_target_pairs={{0,2},{1,3},{2,0},{3,1},{4,6},{5,7},{6,4},{7,5},{8,10},{9,11},{10,... | collective-permute-start | bytes 393224 | tf_op jit(solution)/shard_map/while/body/eval_jaxpr/ppermute | solution.py:27
  212.2 20.4 %collective-permute-start.3 = (bf16[4,8,8,256]{3,2,1,0:T(8,128)(2,1)S(1)}, bf16[4,8,8,256]{3,2,1,0:T(8,128)(2,1)S(1)}, u32[]{:S(2)}, u32[]{:S(2)}) collective-permute-start(bf16[4,8,8,256]{3,2,1,0:T(8,128)(2,1)S(1)} %collective-permute-done.2), channel_id=1, source_target_pairs={{0,4},{1,5},{2,6},{3,7},{4,0},{5,1},{6,2},{7,3},{8,12},{9,13},{10,... | collective-permute-start | bytes 393224 | tf_op jit(solution)/shard_map/while/body/eval_jaxpr/ppermute | solution.py:27
  215.5 17.2 %collective-permute-start = (bf16[4,8,8,256]{3,2,1,0:T(8,128)(2,1)S(1)}, bf16[4,8,8,256]{3,2,1,0:T(8,128)(2,1)S(1)}, u32[]{:S(2)}, u32[]{:S(2)}) collective-permute-start(bf16[4,8,8,256]{3,2,1,0:T(8,128)(2,1)S(1)} %get-tuple-element.1205), channel_id=1, source_target_pairs={{0,1},{1,2},{2,3},{3,4},{4,5},{5,6},{6,7},{8,9},{9,10},{10,11},{11... | collective-permute-start | bytes 393224 | tf_op jit(solution)/shard_map/while/body/eval_jaxpr/ppermute | solution.py:33
  250.8 19.2 %collective-permute-start.3 = (bf16[4,8,8,256]{3,2,1,0:T(8,128)(2,1)S(1)}, bf16[4,8,8,256]{3,2,1,0:T(8,128)(2,1)S(1)}, u32[]{:S(2)}, u32[]{:S(2)}) collective-permute-start(bf16[4,8,8,256]{3,2,1,0:T(8,128)(2,1)S(1)} %collective-permute-done.2), channel_id=1, source_target_pairs={{0,4},{1,5},{2,6},{3,7},{4,0},{5,1},{6,2},{7,3},{8,12},{9,13},{10,... | collective-permute-start | bytes 393224 | tf_op jit(solution)/shard_map/while/body/eval_jaxpr/ppermute | solution.py:27
  274.7 19.8 %collective-permute-start.2 = (bf16[4,8,8,256]{3,2,1,0:T(8,128)(2,1)S(1)}, bf16[4,8,8,256]{3,2,1,0:T(8,128)(2,1)S(1)}, u32[]{:S(2)}, u32[]{:S(2)}) collective-permute-start(bf16[4,8,8,256]{3,2,1,0:T(8,128)(2,1)S(1)} %collective-permute-done.1), channel_id=1, source_target_pairs={{0,2},{1,3},{2,0},{3,1},{4,6},{5,7},{6,4},{7,5},{8,10},{9,11},{10,... | collective-permute-start | bytes 393224 | tf_op jit(solution)/shard_map/while/body/eval_jaxpr/ppermute | solution.py:27
  294.4 18.2 %collective-permute-start.3 = (bf16[4,8,8,256]{3,2,1,0:T(8,128)(2,1)S(1)}, bf16[4,8,8,256]{3,2,1,0:T(8,128)(2,1)S(1)}, u32[]{:S(2)}, u32[]{:S(2)}) collective-permute-start(bf16[4,8,8,256]{3,2,1,0:T(8,128)(2,1)S(1)} %collective-permute-done.2), channel_id=1, source_target_pairs={{0,4},{1,5},{2,6},{3,7},{4,0},{5,1},{6,2},{7,3},{8,12},{9,13},{10,... | collective-permute-start | bytes 393224 | tf_op jit(solution)/shard_map/while/body/eval_jaxpr/ppermute | solution.py:27
  332.6 18.7 %collective-permute-start.3 = (bf16[4,8,8,256]{3,2,1,0:T(8,128)(2,1)S(1)}, bf16[4,8,8,256]{3,2,1,0:T(8,128)(2,1)S(1)}, u32[]{:S(2)}, u32[]{:S(2)}) collective-permute-start(bf16[4,8,8,256]{3,2,1,0:T(8,128)(2,1)S(1)} %collective-permute-done.2), channel_id=1, source_target_pairs={{0,4},{1,5},{2,6},{3,7},{4,0},{5,1},{6,2},{7,3},{8,12},{9,13},{10,... | collective-permute-start | bytes 393224 | tf_op jit(solution)/shard_map/while/body/eval_jaxpr/ppermute | solution.py:27
  357.0 37.8 %collective-permute-start.4 = (bf16[4,8,8,256]{3,2,1,0:T(8,128)(2,1)}, bf16[4,8,8,256]{3,2,1,0:T(8,128)(2,1)}, u32[]{:S(2)}, u32[]{:S(2)}) collective-permute-start(bf16[4,8,8,256]{3,2,1,0:T(8,128)(2,1)} %get-tuple-element.1080), channel_id=1, source_target_pairs={{1,0},{2,1},{3,2},{4,3},{5,4},{6,5},{7,6},{9,8},{10,9},{11,10},{12... | collective-permute-start | bytes 393224 | tf_op jit(solution)/shard_map/while/body/eval_jaxpr/ppermute | solution.py:33
  372.4 22.4 %collective-permute-start.7 = (bf16[4,8,8,256]{3,2,1,0:T(8,128)(2,1)S(1)}, bf16[4,8,8,256]{3,2,1,0:T(8,128)(2,1)S(1)}, u32[]{:S(2)}, u32[]{:S(2)}) collective-permute-start(bf16[4,8,8,256]{3,2,1,0:T(8,128)(2,1)S(1)} %collective-permute-done.6), channel_id=1, source_target_pairs={{0,4},{1,5},{2,6},{3,7},{4,0},{5,1},{6,2},{7,3},{8,12},{9,13},{10,... | collective-permute-start | bytes 393224 | tf_op jit(solution)/shard_map/while/body/eval_jaxpr/ppermute | solution.py:27
  400.0 48.5 %collective-permute-start.4 = (bf16[4,8,8,256]{3,2,1,0:T(8,128)(2,1)}, bf16[4,8,8,256]{3,2,1,0:T(8,128)(2,1)}, u32[]{:S(2)}, u32[]{:S(2)}) collective-permute-start(bf16[4,8,8,256]{3,2,1,0:T(8,128)(2,1)} %get-tuple-element.1080), channel_id=1, source_target_pairs={{1,0},{2,1},{3,2},{4,3},{5,4},{6,5},{7,6},{9,8},{10,9},{11,10},{12... | collective-permute-start | bytes 393224 | tf_op jit(solution)/shard_map/while/body/eval_jaxpr/ppermute | solution.py:33
  418.8 29.6 %collective-permute-start.7 = (bf16[4,8,8,256]{3,2,1,0:T(8,128)(2,1)S(1)}, bf16[4,8,8,256]{3,2,1,0:T(8,128)(2,1)S(1)}, u32[]{:S(2)}, u32[]{:S(2)}) collective-permute-start(bf16[4,8,8,256]{3,2,1,0:T(8,128)(2,1)S(1)} %collective-permute-done.6), channel_id=1, source_target_pairs={{0,4},{1,5},{2,6},{3,7},{4,0},{5,1},{6,2},{7,3},{8,12},{9,13},{10,... | collective-permute-start | bytes 393224 | tf_op jit(solution)/shard_map/while/body/eval_jaxpr/ppermute | solution.py:27
  453.6 45.3 %collective-permute-start.4 = (bf16[4,8,8,256]{3,2,1,0:T(8,128)(2,1)}, bf16[4,8,8,256]{3,2,1,0:T(8,128)(2,1)}, u32[]{:S(2)}, u32[]{:S(2)}) collective-permute-start(bf16[4,8,8,256]{3,2,1,0:T(8,128)(2,1)} %get-tuple-element.1080), channel_id=1, source_target_pairs={{1,0},{2,1},{3,2},{4,3},{5,4},{6,5},{7,6},{9,8},{10,9},{11,10},{12... | collective-permute-start | bytes 393224 | tf_op jit(solution)/shard_map/while/body/eval_jaxpr/ppermute | solution.py:33
  472.3 26.5 %collective-permute-start.7 = (bf16[4,8,8,256]{3,2,1,0:T(8,128)(2,1)S(1)}, bf16[4,8,8,256]{3,2,1,0:T(8,128)(2,1)S(1)}, u32[]{:S(2)}, u32[]{:S(2)}) collective-permute-start(bf16[4,8,8,256]{3,2,1,0:T(8,128)(2,1)S(1)} %collective-permute-done.6), channel_id=1, source_target_pairs={{0,4},{1,5},{2,6},{3,7},{4,0},{5,1},{6,2},{7,3},{8,12},{9,13},{10,... | collective-permute-start | bytes 393224 | tf_op jit(solution)/shard_map/while/body/eval_jaxpr/ppermute | solution.py:27
  504.0 47.0 %collective-permute-start.4 = (bf16[4,8,8,256]{3,2,1,0:T(8,128)(2,1)}, bf16[4,8,8,256]{3,2,1,0:T(8,128)(2,1)}, u32[]{:S(2)}, u32[]{:S(2)}) collective-permute-start(bf16[4,8,8,256]{3,2,1,0:T(8,128)(2,1)} %get-tuple-element.1080), channel_id=1, source_target_pairs={{1,0},{2,1},{3,2},{4,3},{5,4},{6,5},{7,6},{9,8},{10,9},{11,10},{12... | collective-permute-start | bytes 393224 | tf_op jit(solution)/shard_map/while/body/eval_jaxpr/ppermute | solution.py:33
  523.8 27.1 %collective-permute-start.7 = (bf16[4,8,8,256]{3,2,1,0:T(8,128)(2,1)S(1)}, bf16[4,8,8,256]{3,2,1,0:T(8,128)(2,1)S(1)}, u32[]{:S(2)}, u32[]{:S(2)}) collective-permute-start(bf16[4,8,8,256]{3,2,1,0:T(8,128)(2,1)S(1)} %collective-permute-done.6), channel_id=1, source_target_pairs={{0,4},{1,5},{2,6},{3,7},{4,0},{5,1},{6,2},{7,3},{8,12},{9,13},{10,... | collective-permute-start | bytes 393224 | tf_op jit(solution)/shard_map/while/body/eval_jaxpr/ppermute | solution.py:27
  556.0 37.6 %collective-permute-start.4 = (bf16[4,8,8,256]{3,2,1,0:T(8,128)(2,1)}, bf16[4,8,8,256]{3,2,1,0:T(8,128)(2,1)}, u32[]{:S(2)}, u32[]{:S(2)}) collective-permute-start(bf16[4,8,8,256]{3,2,1,0:T(8,128)(2,1)} %get-tuple-element.1080), channel_id=1, source_target_pairs={{1,0},{2,1},{3,2},{4,3},{5,4},{6,5},{7,6},{9,8},{10,9},{11,10},{12... | collective-permute-start | bytes 393224 | tf_op jit(solution)/shard_map/while/body/eval_jaxpr/ppermute | solution.py:33
  575.3 18.2 %collective-permute-start.7 = (bf16[4,8,8,256]{3,2,1,0:T(8,128)(2,1)S(1)}, bf16[4,8,8,256]{3,2,1,0:T(8,128)(2,1)S(1)}, u32[]{:S(2)}, u32[]{:S(2)}) collective-permute-start(bf16[4,8,8,256]{3,2,1,0:T(8,128)(2,1)S(1)} %collective-permute-done.6), channel_id=1, source_target_pairs={{0,4},{1,5},{2,6},{3,7},{4,0},{5,1},{6,2},{7,3},{8,12},{9,13},{10,... | collective-permute-start | bytes 393224 | tf_op jit(solution)/shard_map/while/body/eval_jaxpr/ppermute | solution.py:27
  598.7 55.9 %collective-permute-start.4 = (bf16[4,8,8,256]{3,2,1,0:T(8,128)(2,1)}, bf16[4,8,8,256]{3,2,1,0:T(8,128)(2,1)}, u32[]{:S(2)}, u32[]{:S(2)}) collective-permute-start(bf16[4,8,8,256]{3,2,1,0:T(8,128)(2,1)} %get-tuple-element.1080), channel_id=1, source_target_pairs={{1,0},{2,1},{3,2},{4,3},{5,4},{6,5},{7,6},{9,8},{10,9},{11,10},{12... | collective-permute-start | bytes 393224 | tf_op jit(solution)/shard_map/while/body/eval_jaxpr/ppermute | solution.py:33
  603.5 32.3 %collective-permute-start.6 = (bf16[4,8,8,256]{3,2,1,0:T(8,128)(2,1)S(1)}, bf16[4,8,8,256]{3,2,1,0:T(8,128)(2,1)S(1)}, u32[]{:S(2)}, u32[]{:S(2)}) collective-permute-start(bf16[4,8,8,256]{3,2,1,0:T(8,128)(2,1)S(1)} %collective-permute-done.5), channel_id=1, source_target_pairs={{0,2},{1,3},{2,0},{3,1},{4,6},{5,7},{6,4},{7,5},{8,10},{9,11},{10,... | collective-permute-start | bytes 393224 | tf_op jit(solution)/shard_map/while/body/eval_jaxpr/ppermute | solution.py:27
  635.8 18.7 %collective-permute-start.7 = (bf16[4,8,8,256]{3,2,1,0:T(8,128)(2,1)S(1)}, bf16[4,8,8,256]{3,2,1,0:T(8,128)(2,1)S(1)}, u32[]{:S(2)}, u32[]{:S(2)}) collective-permute-start(bf16[4,8,8,256]{3,2,1,0:T(8,128)(2,1)S(1)} %collective-permute-done.6), channel_id=1, source_target_pairs={{0,4},{1,5},{2,6},{3,7},{4,0},{5,1},{6,2},{7,3},{8,12},{9,13},{10,... | collective-permute-start | bytes 393224 | tf_op jit(solution)/shard_map/while/body/eval_jaxpr/ppermute | solution.py:27
  657.7 18.1 %collective-permute-start.5 = (bf16[4,8,8,256]{3,2,1,0:T(8,128)(2,1)}, bf16[4,8,8,256]{3,2,1,0:T(8,128)(2,1)S(1)}, u32[]{:S(2)}, u32[]{:S(2)}) collective-permute-start(bf16[4,8,8,256]{3,2,1,0:T(8,128)(2,1)} %get-tuple-element.1080), channel_id=1, source_target_pairs={{0,1},{1,0},{2,3},{3,2},{4,5},{5,4},{6,7},{7,6},{8,9},{9,8},{10,11... | collective-permute-start | bytes 393224 | tf_op jit(solution)/shard_map/while/body/eval_jaxpr/ppermute | solution.py:27
  671.0 34.6 %collective-permute-start.4 = (bf16[4,8,8,256]{3,2,1,0:T(8,128)(2,1)}, bf16[4,8,8,256]{3,2,1,0:T(8,128)(2,1)}, u32[]{:S(2)}, u32[]{:S(2)}) collective-permute-start(bf16[4,8,8,256]{3,2,1,0:T(8,128)(2,1)} %get-tuple-element.1080), channel_id=1, source_target_pairs={{1,0},{2,1},{3,2},{4,3},{5,4},{6,5},{7,6},{9,8},{10,9},{11,10},{12... | collective-permute-start | bytes 393224 | tf_op jit(solution)/shard_map/while/body/eval_jaxpr/ppermute | solution.py:33
  688.9 16.7 %collective-permute-start.7 = (bf16[4,8,8,256]{3,2,1,0:T(8,128)(2,1)S(1)}, bf16[4,8,8,256]{3,2,1,0:T(8,128)(2,1)S(1)}, u32[]{:S(2)}, u32[]{:S(2)}) collective-permute-start(bf16[4,8,8,256]{3,2,1,0:T(8,128)(2,1)S(1)} %collective-permute-done.6), channel_id=1, source_target_pairs={{0,4},{1,5},{2,6},{3,7},{4,0},{5,1},{6,2},{7,3},{8,12},{9,13},{10,... | collective-permute-start | bytes 393224 | tf_op jit(solution)/shard_map/while/body/eval_jaxpr/ppermute | solution.py:27
  723.3 34.4 %collective-permute-start.4 = (bf16[4,8,8,256]{3,2,1,0:T(8,128)(2,1)}, bf16[4,8,8,256]{3,2,1,0:T(8,128)(2,1)}, u32[]{:S(2)}, u32[]{:S(2)}) collective-permute-start(bf16[4,8,8,256]{3,2,1,0:T(8,128)(2,1)} %get-tuple-element.1080), channel_id=1, source_target_pairs={{1,0},{2,1},{3,2},{4,3},{5,4},{6,5},{7,6},{9,8},{10,9},{11,10},{12... | collective-permute-start | bytes 393224 | tf_op jit(solution)/shard_map/while/body/eval_jaxpr/ppermute | solution.py:33
  740.5 17.1 %collective-permute-start.7 = (bf16[4,8,8,256]{3,2,1,0:T(8,128)(2,1)S(1)}, bf16[4,8,8,256]{3,2,1,0:T(8,128)(2,1)S(1)}, u32[]{:S(2)}, u32[]{:S(2)}) collective-permute-start(bf16[4,8,8,256]{3,2,1,0:T(8,128)(2,1)S(1)} %collective-permute-done.6), channel_id=1, source_target_pairs={{0,4},{1,5},{2,6},{3,7},{4,0},{5,1},{6,2},{7,3},{8,12},{9,13},{10,... | collective-permute-start | bytes 393224 | tf_op jit(solution)/shard_map/while/body/eval_jaxpr/ppermute | solution.py:27
  983.9 41.7 %collective-permute-start.15 = (f32[16,256]{1,0:T(8,128)S(1)}, f32[16,256]{1,0:T(8,128)S(1)}, u32[]{:S(2)}, u32[]{:S(2)}) collective-permute-start(f32[16,256]{1,0:T(8,128)S(1)} %get-tuple-element.845), channel_id=1, source_target_pairs={{0,8},{8,16},{16,24},{24,32},{32,40},{40,48},{48,56},{56,64},{64,7... | collective-permute-start | bytes 49160
  985.9 41.7 %collective-permute-start.16 = (f32[16,256]{1,0:T(8,128)S(1)}, f32[16,256]{1,0:T(8,128)S(1)}, u32[]{:S(2)}, u32[]{:S(2)}) collective-permute-start(f32[16,256]{1,0:T(8,128)S(1)} %get-tuple-element.845), channel_id=1, source_target_pairs={{0,16},{8,24},{16,32},{24,40},{32,48},{40,56},{48,64},{56,72},{64,... | collective-permute-start | bytes 49160
  987.8 23.4 %collective-permute-start.30 = (f32[12,256]{1,0:T(8,128)S(1)}, f32[12,256]{1,0:T(8,128)S(1)}, u32[]{:S(2)}, u32[]{:S(2)}) collective-permute-start(f32[12,256]{1,0:T(8,128)S(1)} %slice.106), channel_id=1, source_target_pairs={{0,128},{8,136},{16,144},{24,152},{32,160},{40,168},{48,176},{56,1... | collective-permute-start | bytes 36872
  989.1 42.1 %collective-permute-start.17 = (f32[16,256]{1,0:T(8,128)S(1)}, f32[16,256]{1,0:T(8,128)S(1)}, u32[]{:S(2)}, u32[]{:S(2)}) collective-permute-start(f32[16,256]{1,0:T(8,128)S(1)} %get-tuple-element.845), channel_id=1, source_target_pairs={{0,24},{8,32},{16,40},{24,48},{32,56},{40,64},{48,72},{56,80},{64,... | collective-permute-start | bytes 49160
  997.5 35.6 %collective-permute-start.18 = (f32[16,256]{1,0:T(8,128)S(1)}, f32[16,256]{1,0:T(8,128)S(1)}, u32[]{:S(2)}, u32[]{:S(2)}) collective-permute-start(f32[16,256]{1,0:T(8,128)S(1)} %get-tuple-element.845), channel_id=1, source_target_pairs={{0,32},{8,40},{16,48},{24,56},{32,64},{40,72},{48,80},{56,88},{64,... | collective-permute-start | bytes 49160
  1011.2 23.8 %collective-permute-start.19 = (f32[16,256]{1,0:T(8,128)S(1)}, f32[16,256]{1,0:T(8,128)S(1)}, u32[]{:S(2)}, u32[]{:S(2)}) collective-permute-start(f32[16,256]{1,0:T(8,128)S(1)} %get-tuple-element.845), channel_id=1, source_target_pairs={{0,40},{8,48},{16,56},{24,64},{32,72},{40,80},{48,88},{56,96},{64,... | collective-permute-start | bytes 49160
  1040.9 180.1 %collective-permute-start.27 = (f32[16,256]{1,0:T(8,128)S(1)}, f32[16,256]{1,0:T(8,128)S(1)}, u32[]{:S(2)}, u32[]{:S(2)}) collective-permute-start(f32[16,256]{1,0:T(8,128)S(1)} %get-tuple-element.845), channel_id=1, source_target_pairs={{0,104},{8,112},{16,120},{24,128},{32,136},{40,144},{48,152},{56,1... | collective-permute-start | bytes 49160
  1042.8 180.1 %collective-permute-start.28 = (f32[16,256]{1,0:T(8,128)S(1)}, f32[16,256]{1,0:T(8,128)S(1)}, u32[]{:S(2)}, u32[]{:S(2)}) collective-permute-start(f32[16,256]{1,0:T(8,128)S(1)} %get-tuple-element.845), channel_id=1, source_target_pairs={{0,112},{8,120},{16,128},{24,136},{32,144},{40,152},{48,160},{56,1... | collective-permute-start | bytes 49160
  1044.8 191.5 %collective-permute-start.29 = (f32[16,256]{1,0:T(8,128)S(1)}, f32[16,256]{1,0:T(8,128)S(1)}, u32[]{:S(2)}, u32[]{:S(2)}) collective-permute-start(f32[16,256]{1,0:T(8,128)S(1)} %get-tuple-element.845), channel_id=1, source_target_pairs={{0,120},{8,128},{16,136},{24,144},{32,152},{40,160},{48,168},{56,1... | collective-permute-start | bytes 49160
  1046.7 213.9 %collective-permute-start.10 = (f32[40,256]{1,0:T(8,128)S(1)}, f32[40,256]{1,0:T(8,128)S(1)}, u32[]{:S(2)}, u32[]{:S(2)}) collective-permute-start(f32[40,256]{1,0:T(8,128)S(1)} %get-tuple-element.844), channel_id=1, source_target_pairs={{0,24},{8,32},{16,40},{24,48},{32,56},{40,64},{48,72},{56,80},{64,... | collective-permute-start | bytes 122888
  1051.0 207.7 %collective-permute-start.14 = (f32[12,256]{1,0:T(8,128)S(1)}, f32[12,256]{1,0:T(8,128)S(1)}, u32[]{:S(2)}, u32[]{:S(2)}) collective-permute-start(f32[12,256]{1,0:T(8,128)S(1)} %slice.105), channel_id=1, source_target_pairs={{0,56},{8,64},{16,72},{24,80},{32,88},{40,96},{48,104},{56,112},{6... | collective-permute-start | bytes 36872
  1221.0 42.6 %collective-permute-start.11 = (f32[40,256]{1,0:T(8,128)S(1)}, f32[40,256]{1,0:T(8,128)S(1)}, u32[]{:S(2)}, u32[]{:S(2)}) collective-permute-start(f32[40,256]{1,0:T(8,128)S(1)} %get-tuple-element.844), channel_id=1, source_target_pairs={{0,32},{8,40},{16,48},{24,56},{32,64},{40,72},{48,80},{56,88},{64,... | collective-permute-start | bytes 122888
  1222.9 40.7 %collective-permute-start.12 = (f32[40,256]{1,0:T(8,128)S(1)}, f32[40,256]{1,0:T(8,128)S(1)}, u32[]{:S(2)}, u32[]{:S(2)}) collective-permute-start(f32[40,256]{1,0:T(8,128)S(1)} %get-tuple-element.844), channel_id=1, source_target_pairs={{0,40},{8,48},{16,56},{24,64},{32,72},{40,80},{48,88},{56,96},{64,... | collective-permute-start | bytes 122888
  1236.3 27.3 %collective-permute-start.13 = (f32[40,256]{1,0:T(8,128)S(1)}, f32[40,256]{1,0:T(8,128)S(1)}, u32[]{:S(2)}, u32[]{:S(2)}) collective-permute-start(f32[40,256]{1,0:T(8,128)S(1)} %get-tuple-element.844), channel_id=1, source_target_pairs={{0,48},{8,56},{16,64},{24,72},{32,80},{40,88},{48,96},{56,104},{64... | collective-permute-start | bytes 122888
  (120 other events, 1266.0 us)
where the time goes:
time: 1280 us; the launch traced here: 1270 us
  starting transfers between devices  454 us (35%)
  blocking collectives  392 us (31%)
  waiting for transfers between devices  324 us (25%)
  other arithmetic  55.7 us (4%)
  local copies, waits for them, and re-layouts  33.8 us (3%)
    ppermute x48, starting transfers between devices, swapped(): return lax.ppermute(value, axis, pairs)  323 us
    ppermute x48, waiting for transfers between devices, swapped(): return lax.ppermute(value, axis, pairs)  317 us
    unnamed x1, blocking collectives  226 us
    psum x1, blocking collectives, shards(): norm_total = lax.psum(jnp.stack([finished[4], finished[5]]), 'dp')  166 us
    unnamed x23, starting transfers between devices  109 us
    add x8, other arithmetic, backward_tick(): acc_spatial = acc_spatial + result[1]  26.1 us
  transfers between devices with their start and end apart: 87, of which 42 were waited for; matrix products, arithmetic and copies ran while one was open for 3% of the time, Pallas kernels for 0%

commit v1 on v0

v1 whole, which is shorter than its diff:
```python
import functools

import jax
import jax.numpy as jnp
from jax import lax
from jax.experimental import pallas as pl
from jax.experimental.pallas import tpu as pltpu
from jax.sharding import PartitionSpec as P

MESH = pl.DeviceIdType.MESH
EPSILON = 1e-05
CELLS = 256
CH = 256
HALF = 128
SPATIAL = 2304
WEIGHT_ROWS = 3072
SLICE = WEIGHT_ROWS // 16
LONG = WEIGHT_ROWS // 4
SPATIAL_OFFSETS = tuple((dy, dx) for dy in (-1, 0, 1) for dx in (-1, 0, 1))
TEMPORAL_OFFSETS = (-1, 0, 1)
F32 = jnp.float32
BF16 = jnp.bfloat16


def group_mean(value):
    lane = lax.broadcasted_iota(jnp.int32, value.shape, 1)
    for step in (1, 2, 4):
        after = pltpu.roll(value, CH - step, axis=1)
        before = pltpu.roll(value, step, axis=1)
        value = value + jnp.where((lane & step) == 0, after, before)
    return value * 0.125


def over_groups(row_sum):
    wide = jnp.broadcast_to(row_sum * (1.0 / CELLS), (8, CH))
    return group_mean(wide)[0:1]


def shift_x(value, dx):
    if dx == 0:
        return value
    lines = value.reshape(32, 8, CH)
    moved = pltpu.roll(lines, (-dx) % 8, axis=1)
    column = lax.broadcasted_iota(jnp.int32, lines.shape, 1)
    inside = column != (7 if dx == 1 else 0)
    return jnp.where(inside, moved, 0.0).reshape(CELLS, CH)


def shift_y(value, dy):
    if dy == 0:
        return value
    frames = value.reshape(4, 64, CH)
    edge = jnp.zeros((4, 8, CH), value.dtype)
    if dy == 1:
        frames = jnp.concatenate([frames[:, 8:], edge], axis=1)
    else:
        frames = jnp.concatenate([edge, frames[:, :56]], axis=1)
    return frames.reshape(CELLS, CH)


def shift_t(value, dt):
    if dt == 0:
        return value
    edge = jnp.zeros((64, CH), value.dtype)
    if dt == 1:
        return jnp.concatenate([value[64:], edge], axis=0)
    return jnp.concatenate([edge, value[:192]], axis=0)


def fill_spatial(cols, value, sign):
    for dx in (-1, 0, 1):
        moved = shift_x(value, sign * dx)
        for dy in (-1, 0, 1):
            tap = SPATIAL_OFFSETS.index((dy, dx))
            cols[:, tap * CH : (tap + 1) * CH] = shift_y(moved, sign * dy).astype(BF16)


def fill_temporal(cols, value, sign):
    for tap, dt in enumerate(TEMPORAL_OFFSETS):
        cols[:, tap * CH : (tap + 1) * CH] = shift_t(value, sign * dt)


def times_transposed(left, right):
    return lax.dot_general(left, right, (((1,), (1,)), ((), ())), preferred_element_type=F32)


def kernel(
    latents, cotangent, gain_ref, shift_ref, spatial_ref, temporal_ref,
    spatial_out, temporal_out, norm_out,
    wall, prm, hist, ghist, normed_s, slope_s, scale_s, cols, tcols, act_t, mid_t,
    gsend, first_in, first_sum, second_in, third_f, third_out, third_in, norm_acc,
    local_sem, z_send, z_recv, mid_send, mid_recv, last_send, last_recv,
    core_send, core_recv, prm_send, prm_recv,
    g1_send, g1_recv, g2_send, g2_recv, g3_send, g3_recv, n_send, n_recv,
):
    dp = lax.axis_index("dp")
    pos = lax.axis_index("section")
    px = dp // 16
    py = (dp // 4) % 4
    pz = dp % 4
    block = pos // 2
    core = pos % 2

    def at_x(x):
        return (x * 16 + py * 4 + pz, pos)

    def at_y(y):
        return (px * 16 + y * 4 + pz, pos)

    def at_z(z):
        return (px * 16 + py * 4 + z, pos)

    def at_section(s):
        return (dp, s)

    def copy(src, dst, send, recv, device):
        return pltpu.make_async_remote_copy(
            src_ref=src, dst_ref=dst, send_sem=send, recv_sem=recv,
            device_id=device, device_id_type=MESH,
        )

    along = ((px, at_x), (py, at_y))

    loads = [
        pltpu.make_async_copy(spatial_ref.at[0], wall.at[pos, pl.ds(0, SPATIAL)], local_sem.at[0]),
        pltpu.make_async_copy(
            temporal_ref.at[0], wall.at[pos, pl.ds(SPATIAL, WEIGHT_ROWS - SPATIAL)], local_sem.at[1]
        ),
    ]
    for load in loads:
        load.start()

    barrier = pltpu.get_barrier_semaphore()
    for d in (1, 2, 3):
        for mine, place in along + ((pz, at_z),):
            pl.semaphore_signal(
                barrier, inc=1, device_id=place((mine + d) % 4), device_id_type=MESH
            )
    for d in range(1, 8):
        pl.semaphore_signal(
            barrier, inc=1, device_id=at_section((pos + d) % 8), device_id_type=MESH
        )

    rest = jnp.zeros((6, CH), F32)
    prm[pos] = jnp.concatenate([gain_ref[...], shift_ref[...], rest], axis=0)
    hist[0] = latents[...]
    ghist[8] = cotangent[...]
    for load in loads:
        load.wait()
    pl.semaphore_wait(barrier, 16)

    def prm_copy(d):
        return copy(
            prm.at[pos], prm.at[pos], prm_send.at[d], prm_recv.at[pos], at_section((pos + d) % 8)
        )

    def prm_arrival(d):
        other = (pos + d) % 8
        return copy(prm.at[other], prm.at[other], prm_send.at[d], prm_recv.at[other], at_section(other))

    for d in range(1, 8):
        prm_copy(d).start()

    def core_copy(pair):
        section = 2 * pair + core
        return copy(
            wall.at[section], wall.at[section], core_send.at[pair], core_recv.at[pair],
            at_section(block * 2 + 1 - core),
        )

    def core_arrival(pair):
        section = 2 * pair + 1 - core
        return copy(
            wall.at[section], wall.at[section], core_send.at[pair], core_recv.at[pair],
            at_section(block * 2 + 1 - core),
        )

    core_copy(block).start()

    def part(section, row, rows, half):
        return wall.at[section, pl.ds(row, rows), pl.ds(half * HALF, HALF)]

    slice_row = ((py * 4 + px) * SLICE, (px * 4 + py) * SLICE)
    long_row = (py * LONG, px * LONG)

    def z_copy(d, half):
        target = (block + d) % 4
        order = jnp.where(block < target, block, block - 1)
        ref = part(pos, slice_row[half], SLICE, half)
        return copy(
            ref, ref, z_send.at[d, half], z_recv.at[order, half], at_section(target * 2 + core)
        )

    for d in (1, 3, 2):
        for half in (0, 1):
            z_copy(d, half).start()

    def pair_of(k):
        return jnp.where(k < block, k, k + 1)

    def z_arrival(k, half):
        section = 2 * pair_of(k) + core
        ref = part(section, slice_row[half], SLICE, half)
        return copy(ref, ref, z_send.at[1, half], z_recv.at[k, half], at_section((pos + 2) % 8))

    def mid_copy(k, half, d):
        mine, place = along[half]
        ref = part(2 * pair_of(k) + core, slice_row[half], SLICE, half)
        return copy(
            ref, ref, mid_send.at[k, half, d], mid_recv.at[k, half, mine], place((mine + d) % 4)
        )

    def mid_arrival(k, half, d):
        mine, place = along[half]
        source = (mine + d) % 4
        row = long_row[half] + source * SLICE
        ref = part(2 * pair_of(k) + core, row, SLICE, half)
        return copy(ref, ref, mid_send.at[k, half, d], mid_recv.at[k, half, source], place(source))

    def last_copy(k, half, d):
        mine, place = along[1 - half]
        ref = part(2 * pair_of(k) + core, long_row[half], LONG, half)
        return copy(
            ref, ref, last_send.at[k, half, d], last_recv.at[k, half, mine], place((mine + d) % 4)
        )

    def last_arrival(k, half, d):
        mine, place = along[1 - half]
        source = (mine + d) % 4
        ref = part(2 * pair_of(k) + core, source * LONG, LONG, half)
        return copy(ref, ref, last_send.at[k, half, d], last_recv.at[k, half, source], place(source))

    def spread(k, carry):
        for half in (0, 1):
            z_arrival(k, half).wait_recv()
            for d in (1, 3, 2):
                mid_copy(k, half, d).start()
        for half in (0, 1):
            for d in (1, 3, 2):
                mid_arrival(k, half, d).wait_recv()
            for d in (1, 3, 2):
                last_copy(k, half, d).start()
        return carry

    def forward(s):
        params = prm[s]
        gain = params[0:1]
        shift = params[1:2]
        decoder = s >= 4
        skip = jnp.where(decoder, 1.0, 0.0)
        inputs = hist[s].astype(F32) + skip * hist[jnp.where(decoder, 8 - s, 0)].astype(F32)
        center = over_groups(jnp.sum(inputs, axis=0, keepdims=True))
        deviation = inputs - center
        variance = over_groups(jnp.sum(deviation * deviation, axis=0, keepdims=True))
        scaling = lax.rsqrt(variance + EPSILON)
        normed = deviation * scaling
        before = normed * gain + shift
        sigma = jax.nn.sigmoid(before)
        normed_s[s] = normed
        slope_s[s] = sigma * (1.0 + before * (1.0 - sigma))
        scale_s[s] = jnp.broadcast_to(scaling, (8, CH))

        @pl.when((s < 7) | (pos == 7))
        def _():
            active = before * sigma
            fill_spatial(cols, active, 1)
            middle = jnp.dot(cols[...], wall[s, 0:SPATIAL], preferred_element_type=F32)
            rounded = middle.astype(BF16)
            fill_temporal(tcols, rounded, 1)
            branch = jnp.dot(tcols[...], wall[s, SPATIAL:WEIGHT_ROWS], preferred_element_type=F32)
            hist[s + 1] = (inputs + branch).astype(BF16)

            @pl.when(s == pos)
            def _():
                act_t[...] = active.T.astype(BF16)
                mid_t[...] = middle.T.astype(BF16)

    def forward_pair(pair, carry):
        @pl.when(pair == jnp.where(block == 0, 1, 0))
        def _():
            lax.fori_loop(0, 3, spread, 0)

        @pl.when(pair != block)
        def _():
            k = jnp.where(pair < block, pair, pair - 1)
            for half in (0, 1):
                for d in (1, 3, 2):
                    last_arrival(k, half, d).wait_recv()
            core_copy(pair).start()

        @pl.when(pair == 0)
        def _():
            for d in range(1, 8):
                prm_arrival(d).wait_recv()

        core_arrival(pair).wait_recv()

        def one(index, inner):
            forward(2 * pair + index)
            return inner

        return lax.fori_loop(0, 2, one, carry)

    lax.fori_loop(0, 4, forward_pair, 0)

    def upstream(s):
        encoder = s < 4
        extra = jnp.where(encoder, 1.0, 0.0)
        other = ghist[jnp.where(encoder, 7 - s, 8)].astype(F32)
        return (ghist[s + 1].astype(F32) + extra * other).astype(BF16)

    def middle_grad(s, up):
        fill_temporal(tcols, up, -1)
        total = jnp.zeros((CELLS, CH), F32)
        for tap in range(3):
            weight = wall[s, SPATIAL + tap * CH : SPATIAL + (tap + 1) * CH]
            total = total + times_transposed(tcols[:, tap * CH : (tap + 1) * CH], weight)
        fill_spatial(cols, total, -1)

    def before_grad(s):
        total = jnp.zeros((CELLS, CH), F32)
        for tap in range(9):
            weight = wall[s, tap * CH : (tap + 1) * CH]
            total = total + times_transposed(cols[:, tap * CH : (tap + 1) * CH], weight)
        return total * slope_s[s]

    def backward(i, carry):
        s = 7 - i
        gain = prm[s][0:1]
        up = upstream(s)
        middle_grad(s, up)
        grad = before_grad(s)
        normed = normed_s[s]
        inner = over_groups(gain * jnp.sum(grad, axis=0, keepdims=True))
        project = over_groups(gain * jnp.sum(grad * normed, axis=0, keepdims=True))
        input_grad = scale_s[s][0:1] * (grad * gain - inner - normed * project)
        ghist[s] = (up.astype(F32) + input_grad).astype(BF16)
        return carry

    lax.fori_loop(0, 7 - pos, backward, 0)

    def store_rows(tile, row, per_x, per_y, base):
        end = row + CH
        while row < end:
            stop = min(end, (row // per_y + 1) * per_y)
            where_x = row // per_x
            where_y = (row % per_x) // per_y
            inside = row % per_y
            start = CH - (end - row)
            gsend[where_x, where_y, base + inside : base + inside + stop - row, :] = tile[
                start : start + stop - row
            ]
            row = stop

    up = upstream(pos)
    middle_grad(pos, up)
    for tap in range(3):
        tile = jnp.dot(mid_t[...], tcols[:, tap * CH : (tap + 1) * CH], preferred_element_type=F32)
        store_rows(tile.astype(BF16), tap * CH, 192, 48, 144)
    for tap in range(9):
        tile = jnp.dot(act_t[...], cols[:, tap * CH : (tap + 1) * CH], preferred_element_type=F32)
        store_rows(tile.astype(BF16), tap * CH, 576, 144, 0)

    def own_part(half, index):
        if half == 0:
            return gsend.at[index, :, :, pl.ds(0, HALF)]
        return gsend.at[:, index, :, pl.ds(HALF, HALF)]

    def g1_copy(half, d):
        mine, place = along[half]
        target = (mine + d) % 4
        return copy(
            own_part(half, target), first_in.at[half, mine], g1_send.at[half, d],
            g1_recv.at[half, mine], place(target),
        )

    def g1_arrival(half, d):
        mine, place = along[half]
        source = (mine + d) % 4
        return copy(
            own_part(half, source), first_in.at[half, source], g1_send.at[half, d],
            g1_recv.at[half, source], place(source),
        )

    def g2_copy(half, d):
        mine, place = along[1 - half]
        target = (mine + d) % 4
        return copy(
            first_sum.at[half, target], second_in.at[half, mine], g2_send.at[half, d],
            g2_recv.at[half, mine], place(target),
        )

    def g2_arrival(half, d):
        mine, place = along[1 - half]
        source = (mine + d) % 4
        return copy(
            first_sum.at[half, source], second_in.at[half, source], g2_send.at[half, d],
            g2_recv.at[half, source], place(source),
        )

    def g3_copy(d):
        target = (pz + d) % 4
        return copy(
            third_out.at[target], third_in.at[pz], g3_send.at[d], g3_recv.at[pz], at_z(target)
        )

    def g3_arrival(d):
        source = (pz + d) % 4
        return copy(
            third_out.at[source], third_in.at[source], g3_send.at[d], g3_recv.at[source], at_z(source)
        )

    for half in (0, 1):
        for d in (1, 3, 2):
            g1_copy(half, d).start()

    axes = along + ((pz, at_z),)

    def n_copy(phase, d):
        mine, place = axes[phase]
        return copy(
            norm_acc.at[phase, mine], norm_acc.at[phase, mine], n_send.at[phase, d],
            n_recv.at[phase, mine], place((mine + d) % 4),
        )

    def n_arrival(phase, d):
        mine, place = axes[phase]
        source = (mine + d) % 4
        return copy(
            norm_acc.at[phase, source], norm_acc.at[phase, source], n_send.at[phase, d],
            n_recv.at[phase, source], place(source),
        )

    grad = before_grad(pos)
    gain_term = jnp.sum(grad * normed_s[pos], axis=0, keepdims=True)
    shift_term = jnp.sum(grad, axis=0, keepdims=True)
    norm_value = jnp.concatenate([gain_term, shift_term, rest], axis=0)

    def norm_start(phase, value):
        norm_acc[phase, axes[phase][0]] = value
        for d in (1, 3, 2):
            n_copy(phase, d).start()

    def norm_finish(phase):
        for d in (1, 3, 2):
            n_arrival(phase, d).wait_recv()
        return ((norm_acc[phase, 0] + norm_acc[phase, 1]) + norm_acc[phase, 2]) + norm_acc[phase, 3]

    norm_start(0, norm_value)

    for half in (0, 1):
        mine = along[half][0]
        for d in (1, 3, 2):
            g1_arrival(half, d).wait_recv()
        for index in range(4):
            if half == 0:
                total = gsend[mine, index, :, 0:HALF].astype(F32)
            else:
                total = gsend[index, mine, :, HALF:CH].astype(F32)
            for d in (1, 2, 3):
                total = total + first_in[half, (mine + d) % 4, index].astype(F32)
            first_sum[half, index] = total.astype(BF16)
        for d in (1, 3, 2):
            g2_copy(half, d).start()

    norm_start(1, norm_finish(0))

    for half in (0, 1):
        mine = along[1 - half][0]
        for d in (1, 3, 2):
            g2_arrival(half, d).wait_recv()
        total = first_sum[half, mine].astype(F32)
        for d in (1, 2, 3):
            total = total + second_in[half, (mine + d) % 4].astype(F32)
        columns = slice(half * HALF, (half + 1) * HALF)
        for z in range(4):
            third_f[z, 0:36, columns] = total[z * 36 : (z + 1) * 36]
            third_f[z, 36:48, columns] = total[144 + z * 12 : 144 + (z + 1) * 12]
    for z in range(4):
        third_out[z] = third_f[z].astype(BF16)
    for d in (1, 3, 2):
        g3_copy(d).start()

    norm_start(2, norm_finish(1))

    total = third_f[pz]
    for d in (1, 3, 2):
        g3_arrival(d).wait_recv()
    for d in (1, 2, 3):
        total = total + third_in[(pz + d) % 4].astype(F32)
    spatial_out[0] = total[0:36]
    temporal_out[0] = total[36:48]
    norm_out[0] = norm_finish(2)[0:2]

    for d in range(1, 8):
        prm_copy(d).wait_send()
    for d in (1, 3, 2):
        for half in (0, 1):
            z_copy(d, half).wait_send()
            g1_copy(half, d).wait_send()
            g2_copy(half, d).wait_send()
        g3_copy(d).wait_send()
        for phase in range(3):
            n_copy(phase, d).wait_send()
    for k in range(3):
        for half in (0, 1):
            for d in (1, 3, 2):
                mid_copy(k, half, d).wait_send()
                last_copy(k, half, d).wait_send()
    for pair in range(4):
        core_copy(pair).wait_send()


def shards(latents, cotangent, spatial_weight, temporal_weight, norm_gain, norm_shift):
    vmem = pl.BlockSpec(memory_space=pltpu.VMEM)
    anywhere = pl.BlockSpec(memory_space=pl.ANY)
    dma = pltpu.SemaphoreType.DMA
    return pl.pallas_call(
        kernel,
        out_shape=(
            jax.ShapeDtypeStruct((1, 36, CH), F32),
            jax.ShapeDtypeStruct((1, 12, CH), F32),
            jax.ShapeDtypeStruct((1, 2, CH), F32),
        ),
        in_specs=[vmem, vmem, vmem, vmem, anywhere, anywhere],
        out_specs=(vmem, vmem, vmem),
        scratch_shapes=[
            pltpu.VMEM((8, WEIGHT_ROWS, CH), BF16),
            pltpu.VMEM((8, 8, CH), F32),
            pltpu.VMEM((9, CELLS, CH), BF16),
            pltpu.VMEM((9, CELLS, CH), BF16),
            pltpu.VMEM((8, CELLS, CH), F32),
            pltpu.VMEM((8, CELLS, CH), F32),
            pltpu.VMEM((8, 8, CH), F32),
            pltpu.VMEM((CELLS, SPATIAL), BF16),
            pltpu.VMEM((CELLS, 3 * CH), BF16),
            pltpu.VMEM((CH, CELLS), BF16),
            pltpu.VMEM((CH, CELLS), BF16),
            pltpu.VMEM((4, 4, 192, CH), BF16),
            pltpu.VMEM((2, 4, 4, 192, HALF), BF16),
            pltpu.VMEM((2, 4, 192, HALF), BF16),
            pltpu.VMEM((2, 4, 192, HALF), BF16),
            pltpu.VMEM((4, 48, CH), F32),
            pltpu.VMEM((4, 48, CH), BF16),
            pltpu.VMEM((4, 48, CH), BF16),
            pltpu.VMEM((3, 4, 8, CH), F32),
            dma((2,)),
            dma((4, 2)), dma((3, 2)),
            dma((3, 2, 4)), dma((3, 2, 4)),
            dma((3, 2, 4)), dma((3, 2, 4)),
            dma((4,)), dma((4,)),
            dma((8,)), dma((8,)),
            dma((2, 4)), dma((2, 4)),
            dma((2, 4)), dma((2, 4)),
            dma((4,)), dma((4,)),
            dma((3, 4)), dma((3, 4)),
        ],
        compiler_params=pltpu.CompilerParams(
            collective_id=0, has_side_effects=True, vmem_limit_bytes=56 * 1024 * 1024
        ),
        cost_estimate=pl.CostEstimate(
            flops=2 * 256 * 256 * 3072 * 17, bytes_accessed=4 * 1024 * 1024, transcendentals=8 * 65536
        ),
    )(
        latents.reshape(CELLS, CH), cotangent.reshape(CELLS, CH), norm_gain, norm_shift,
        spatial_weight, temporal_weight,
    )


def solution(mesh):
    return jax.shard_map(
        shards,
        mesh=mesh,
        in_specs=(
            P("dp", None, None, None, None),
            P("dp", None, None, None, None),
            P("section", None, None),
            P("section", None, None),
            P("section", None),
            P("section", None),
        ),
        out_specs=(P("section", "dp", None), P("section", "dp", None), P("section", None, None)),
        check_vma=False,
    )
```

time: 1280 us -> 118 us (0.09)
  the two profiles are of different devices: /device:TPU:6 before, /device:TPU:129 now
where the time goes in v1:
time: 118 us
  Pallas kernels  113 us (96%)
  local copies, waits for them, and re-layouts  4 us (3%)
    pallas_call x1, Pallas kernels, shards(): pl.pallas_call(kernel, out_shape=(jax.ShapeDtypeStruct((1, 36, CH), F32),...  113 us
    pallas_call x2, local copies, waits for them, and re-layouts, shards(): pl.pallas_call(kernel, out_shape=(jax.ShapeDtypeStruct((1, 36, CH), F32),...  2.76 us

profile of v1, /device:TPU:129, one launch (start us, length us, event | category | flops | bytes accessed | tf_op | source)
XLA Modules:
  0.0 117.7 jit_solution(3925736242888336552)
XLA Ops:
  0.6 113.0 %shard_map.85 = (f32[1,36,256]{2,1,0:T(8,128)}, f32[1,12,256]{2,1,0:T(8,128)}, f32[1,2,256]{2,1,0:T(2,128)}) custom-call(bf16[256,256]{1,0:T(8,128)(2,1)} %bitcast.2, bf16[256,256]{1,0:T(8,128)(2,1)} %bitcast.3, f32[1,256]{1,0:T(1,128)} %gain_ref.1, f32[1,256]{1,0:T(1,128)} %shift_ref.1, bf16[1,2304,256]{2,1,0:T(8,128)(2,1)} %spatial_ref.1, ...), custom_call_target="tpu_custom_call" | custom-call | flops 6845104128 | bytes 4194304 | tf_op jit(solution)/shard_map/pallas_call | solution.py:518
  113.7 1.4 %copy.9 = f32[1,36,256]{2,0,1:T(1,128)} copy(f32[1,36,256]{2,1,0:T(8,128)} %get-tuple-element.3) | data formatting | bytes 73728 | tf_op jit(solution)/shard_map/pallas_call | solution.py:518
  115.1 1.3 %copy.10 = f32[1,12,256]{2,0,1:T(1,128)} copy(f32[1,12,256]{2,1,0:T(8,128)} %get-tuple-element.4) | data formatting | bytes 24576 | tf_op jit(solution)/shard_map/pallas_call | solution.py:518
  116.4 1.2 %copy.12 = f32[1,2,256]{2,1,0:T(2,128)} copy(f32[1,2,256]{2,1,0:T(2,128)} %get-tuple-element.11) | data formatting | bytes 4096

commit v2 on v1

--- a/solution.py
+++ b/solution.py
@@ -16,6 +16,7 @@
 WEIGHT_ROWS = 3072
 SLICE = WEIGHT_ROWS // 16
 LONG = WEIGHT_ROWS // 4
+BIT = SLICE // 4
 SPATIAL_OFFSETS = tuple((dy, dx) for dy in (-1, 0, 1) for dx in (-1, 0, 1))
 TEMPORAL_OFFSETS = (-1, 0, 1)
 F32 = jnp.float32
@@ -86,11 +87,12 @@
 
 def kernel(
     latents, cotangent, gain_ref, shift_ref, spatial_ref, temporal_ref,
-    spatial_out, temporal_out, norm_out,
+    packed_out,
     wall, prm, hist, ghist, normed_s, slope_s, scale_s, cols, tcols, act_t, mid_t,
     gsend, first_in, first_sum, second_in, third_f, third_out, third_in, norm_acc,
-    local_sem, z_send, z_recv, mid_send, mid_recv, last_send, last_recv,
-    core_send, core_recv, prm_send, prm_recv,
+    local_sem, own_send, own_recv, z_send, z_recv, relay_send, line_send, line_recv,
+    mid_send, mid_recv, last_send, last_recv, far_send, far_recv, core_send, core_recv,
+    prm_send, prm_recv, prm_core_send, prm_core_recv,
     g1_send, g1_recv, g2_send, g2_recv, g3_send, g3_recv, n_send, n_recv,
 ):
     dp = lax.axis_index("dp")
@@ -136,9 +138,9 @@
             pl.semaphore_signal(
                 barrier, inc=1, device_id=place((mine + d) % 4), device_id_type=MESH
             )
-    for d in range(1, 8):
+    for other in (pos + 2, pos + 6, pos + 1 - 2 * core):
         pl.semaphore_signal(
-            barrier, inc=1, device_id=at_section((pos + d) % 8), device_id_type=MESH
+            barrier, inc=1, device_id=at_section(other % 8), device_id_type=MESH
         )
 
     rest = jnp.zeros((6, CH), F32)
@@ -147,100 +149,262 @@
     ghist[8] = cotangent[...]
     for load in loads:
         load.wait()
-    pl.semaphore_wait(barrier, 16)
-
-    def prm_copy(d):
-        return copy(
-            prm.at[pos], prm.at[pos], prm_send.at[d], prm_recv.at[pos], at_section((pos + d) % 8)
-        )
-
-    def prm_arrival(d):
-        other = (pos + d) % 8
-        return copy(prm.at[other], prm.at[other], prm_send.at[d], prm_recv.at[other], at_section(other))
-
-    for d in range(1, 8):
-        prm_copy(d).start()
-
-    def core_copy(pair):
-        section = 2 * pair + core
-        return copy(
-            wall.at[section], wall.at[section], core_send.at[pair], core_recv.at[pair],
-            at_section(block * 2 + 1 - core),
-        )
-
-    def core_arrival(pair):
-        section = 2 * pair + 1 - core
-        return copy(
-            wall.at[section], wall.at[section], core_send.at[pair], core_recv.at[pair],
-            at_section(block * 2 + 1 - core),
-        )
-
-    core_copy(block).start()
+    pl.semaphore_wait(barrier, 12)
+
+    other_core = at_section(pos + 1 - 2 * core)
+    after = (block + 1) % 4
+    behind = (block + 3) % 4
+
+    def order(pair, seen_from):
+        return jnp.where(pair < seen_from, pair, pair - 1)
+
+    def pair_of(k):
+        return jnp.where(k < block, k, k + 1)
+
+    def section_of(k):
+        return 2 * pair_of(k) + core
 
     def part(section, row, rows, half):
         return wall.at[section, pl.ds(row, rows), pl.ds(half * HALF, HALF)]
 
-    slice_row = ((py * 4 + px) * SLICE, (px * 4 + py) * SLICE)
-    long_row = (py * LONG, px * LONG)
-
-    def z_copy(d, half):
-        target = (block + d) % 4
-        order = jnp.where(block < target, block, block - 1)
-        ref = part(pos, slice_row[half], SLICE, half)
-        return copy(
-            ref, ref, z_send.at[d, half], z_recv.at[order, half], at_section(target * 2 + core)
-        )
-
-    for d in (1, 3, 2):
-        for half in (0, 1):
-            z_copy(d, half).start()
-
-    def pair_of(k):
-        return jnp.where(k < block, k, k + 1)
+    def slice_row(m, n):
+        return (n * 4 + m) * SLICE
+
+    def own_copy():
+        return copy(wall.at[pos], wall.at[pos], own_send.at[0], own_recv.at[0], other_core)
+
+    def own_arrival():
+        ref = wall.at[pos + 1 - 2 * core]
+        return copy(ref, ref, own_send.at[0], own_recv.at[0], other_core)
+
+    def bit(section, half, line):
+        m, n = along[half][0], along[1 - half][0]
+        return part(section, slice_row(m, n) + line * BIT, BIT, half)
+
+    targets = (after, behind)
+
+    def z_copy(way, half):
+        target = targets[way]
+        ref = bit(pos, half, pz)
+        return copy(
+            ref, ref, z_send.at[way, half], z_recv.at[order(block, target), half],
+            at_section(target * 2 + core),
+        )
 
     def z_arrival(k, half):
-        section = 2 * pair_of(k) + core
-        ref = part(section, slice_row[half], SLICE, half)
-        return copy(ref, ref, z_send.at[1, half], z_recv.at[k, half], at_section((pos + 2) % 8))
-
-    def mid_copy(k, half, d):
-        mine, place = along[half]
-        ref = part(2 * pair_of(k) + core, slice_row[half], SLICE, half)
-        return copy(
-            ref, ref, mid_send.at[k, half, d], mid_recv.at[k, half, mine], place((mine + d) % 4)
-        )
-
-    def mid_arrival(k, half, d):
-        mine, place = along[half]
-        source = (mine + d) % 4
-        row = long_row[half] + source * SLICE
-        ref = part(2 * pair_of(k) + core, row, SLICE, half)
-        return copy(ref, ref, mid_send.at[k, half, d], mid_recv.at[k, half, source], place(source))
-
-    def last_copy(k, half, d):
-        mine, place = along[1 - half]
-        ref = part(2 * pair_of(k) + core, long_row[half], LONG, half)
-        return copy(
-            ref, ref, last_send.at[k, half, d], last_recv.at[k, half, mine], place((mine + d) % 4)
-        )
-
-    def last_arrival(k, half, d):
-        mine, place = along[1 - half]
-        source = (mine + d) % 4
-        ref = part(2 * pair_of(k) + core, source * LONG, LONG, half)
-        return copy(ref, ref, last_send.at[k, half, d], last_recv.at[k, half, source], place(source))
-
-    def spread(k, carry):
+        ref = bit(section_of(k), half, pz)
+        return copy(ref, ref, z_send.at[0, half], z_recv.at[k, half], at_section(after * 2 + core))
+
+    def relay_copy(way):
+        pair, target = (behind, after) if way == 0 else (after, behind)
+        ref = bit(2 * pair + core, way, pz)
+        return copy(
+            ref, ref, relay_send.at[way], z_recv.at[order(pair, target), way],
+            at_section(target * 2 + core),
+        )
+
+    def prm_copy(way):
+        section = 2 * behind + core if way == 2 else pos
+        target = after if way == 2 else targets[way]
+        pair = behind if way == 2 else block
+        return copy(
+            prm.at[section], prm.at[section], prm_send.at[way], prm_recv.at[order(pair, target)],
+            at_section(target * 2 + core),
+        )
+
+    def prm_arrival(k):
+        ref = prm.at[section_of(k)]
+        return copy(ref, ref, prm_send.at[0], prm_recv.at[k], at_section(after * 2 + core))
+
+    def prm_core_copy(pair):
+        ref = prm.at[2 * pair + core]
+        return copy(ref, ref, prm_core_send.at[pair], prm_core_recv.at[pair], other_core)
+
+    def prm_core_arrival(pair):
+        ref = prm.at[2 * pair + 1 - core]
+        return copy(ref, ref, prm_core_send.at[pair], prm_core_recv.at[pair], other_core)
+
+    def line_copy(k, half, d):
+        ref = bit(section_of(k), half, pz)
+        return copy(
+            ref, ref, line_send.at[k, half, d], line_recv.at[k, half, pz], at_z((pz + d) % 4)
+        )
+
+    def line_arrival(k, half, d):
+        source = (pz + d) % 4
+        ref = bit(section_of(k), half, source)
+        return copy(ref, ref, line_send.at[k, half, d], line_recv.at[k, half, source], at_z(source))
+
+    def mid_copy(k, half, slot, arrival=False):
+        (m, place), n = along[half], along[1 - half][0]
+        step = 1 if slot % 2 == 0 else 3
+        if arrival:
+            step = 4 - step
+        target = place((m + step) % 4)
+        if slot < 2:
+            source = (m + step) % 4 if arrival else m
+            row, rows = slice_row(source, n), SLICE
+        else:
+            source = (m + 2) % 4 if arrival else (m + 4 - step) % 4
+            row, rows = slice_row(source, n) + (slot - 2) * (SLICE // 2), SLICE // 2
+        ref = part(section_of(k), row, rows, half)
+        return copy(ref, ref, mid_send.at[k, half, slot], mid_recv.at[k, half, slot], target)
+
+    def last_copy(k, half, way, index, arrival=False):
+        m, (n, place) = along[half][0], along[1 - half]
+        step = 1 if way == 0 else 3
+        if arrival:
+            step = 4 - step
+        slab = (n + step) % 4 if arrival else n
+        row = slice_row((m + (0, 3, 1, 2)[index]) % 4, slab)
+        ref = part(section_of(k), row, SLICE, half)
+        return copy(
+            ref, ref, last_send.at[k, half, way, index], last_recv.at[k, half, way, index],
+            place((n + step) % 4),
+        )
+
+    def far_copy(k, half, index, arrival=False):
+        m, (n, place) = along[half][0], along[1 - half]
+        step = 1 if index < 2 else 3
+        if arrival:
+            step = 4 - step
+        slab = (n + 2) % 4 if arrival else (n + 4 - step) % 4
+        row = slice_row((m + (0, 3, 1, 2)[index]) % 4, slab)
+        ref = part(section_of(k), row, SLICE, half)
+        return copy(
+            ref, ref, far_send.at[k, half, index], far_recv.at[k, half, index],
+            place((n + step) % 4),
+        )
+
+    def core_copy(k, half, index, arrival=False):
+        n = along[1 - half][0]
+        section = 2 * pair_of(k) + (1 - core if arrival else core)
+        ref = part(section, ((n + (0, 3, 1, 2)[index]) % 4) * LONG, LONG, half)
+        return copy(
+            ref, ref, core_send.at[k, half, index], core_recv.at[k, half, index], other_core
+        )
+
+    def act_a(pair, relay):
+        k = order(pair, block)
         for half in (0, 1):
             z_arrival(k, half).wait_recv()
+            if relay == half:
+                relay_copy(half).start()
             for d in (1, 3, 2):
-                mid_copy(k, half, d).start()
+                line_copy(k, half, d).start()
+        prm_arrival(k).wait_recv()
+        if relay == 0:
+            prm_copy(2).start()
+        prm_core_copy(pair).start()
+
+    def act_b(k):
         for half in (0, 1):
             for d in (1, 3, 2):
-                mid_arrival(k, half, d).wait_recv()
-            for d in (1, 3, 2):
-                last_copy(k, half, d).start()
-        return carry
+                line_arrival(k, half, d).wait_recv()
+            for slot in (0, 1):
+                mid_copy(k, half, slot).start()
+            for way in (0, 1):
+                last_copy(k, half, way, 0).start()
+
+    def act_c(k):
+        for half in (0, 1):
+            for slot in (0, 1):
+                mid_copy(k, half, slot, True).wait_recv()
+            for slot in (2, 3):
+                mid_copy(k, half, slot).start()
+            for index in (1, 2):
+                for way in (0, 1):
+                    last_copy(k, half, way, index).start()
+
+    def act_d(k):
+        for half in (0, 1):
+            for slot in (2, 3):
+                mid_copy(k, half, slot, True).wait_recv()
+            for way in (0, 1):
+                last_copy(k, half, way, 3).start()
+            core_copy(k, half, 0).start()
+
+    def act_e(k):
+        for half in (0, 1):
+            for index in (0, 1):
+                last_copy(k, half, 0, index, True).wait_recv()
+                far_copy(k, half, index).start()
+            for index in (2, 3):
+                last_copy(k, half, 1, index, True).wait_recv()
+                far_copy(k, half, index).start()
+
+    def act_f(k):
+        for half in (0, 1):
+            for index in (2, 3):
+                last_copy(k, half, 0, index, True).wait_recv()
+            core_copy(k, half, 1).start()
+            for index in (0, 1):
+                last_copy(k, half, 1, index, True).wait_recv()
+            core_copy(k, half, 2).start()
+
+    def act_g(k):
+        for half in (0, 1):
+            for index in range(4):
+                far_copy(k, half, index, True).wait_recv()
+            core_copy(k, half, 3).start()
+
+    def act_h(k):
+        for half in (0, 1):
+            for index in range(4):
+                core_copy(k, half, index, True).wait_recv()
+        prm_core_arrival(pair_of(k)).wait_recv()
+
+    for half in (0, 1):
+        for way in (0, 1):
+            z_copy(way, half).start()
+    for way in (0, 1):
+        prm_copy(way).start()
+    prm_core_copy(block).start()
+    own_copy().start()
+
+    def gather_start():
+        act_a(behind, 0)
+        act_a(after, 1)
+        far_first = block == 2
+        pl.when(jnp.logical_not(far_first))(lambda: act_b(0))
+        act_a((block + 2) % 4, None)
+        pl.when(far_first)(lambda: act_b(0))
+        act_b(1)
+        act_c(0)
+        act_d(0)
+        act_c(1)
+        act_e(0)
+        act_b(2)
+        act_d(1)
+        act_f(0)
+        act_c(2)
+        act_g(0)
+        act_e(1)
+        act_d(2)
+
+    def gather_sent():
+        def one(k, carry):
+            for half in (0, 1):
+                for d in (1, 3, 2):
+                    line_copy(k, half, d).wait_send()
+                for index in range(4):
+                    mid_copy(k, half, index).wait_send()
+                    for way in (0, 1):
+                        last_copy(k, half, way, index).wait_send()
+                    far_copy(k, half, index).wait_send()
+                    core_copy(k, half, index).wait_send()
+            return carry
+
+        for half in (0, 1):
+            for way in (0, 1):
+                z_copy(way, half).wait_send()
+            relay_copy(half).wait_send()
+        for way in range(3):
+            prm_copy(way).wait_send()
+        for pair in range(4):
+            prm_core_copy(pair).wait_send()
+        own_copy().wait_send()
+        lax.fori_loop(0, 3, one, 0)
 
     def forward(s):
         params = prm[s]
@@ -276,27 +440,37 @@
                 mid_t[...] = middle.T.astype(BF16)
 
     def forward_pair(pair, carry):
+        foreign = pair != block
+        k = order(pair, block)
+
         @pl.when(pair == jnp.where(block == 0, 1, 0))
         def _():
-            lax.fori_loop(0, 3, spread, 0)
-
-        @pl.when(pair != block)
+            gather_start()
+
+        @pl.when(foreign)
         def _():
-            k = jnp.where(pair < block, pair, pair - 1)
-            for half in (0, 1):
-                for d in (1, 3, 2):
-                    last_arrival(k, half, d).wait_recv()
-            core_copy(pair).start()
-
-        @pl.when(pair == 0)
+            act_h(k)
+
+        @pl.when(pair == block)
         def _():
-            for d in range(1, 8):
-                prm_arrival(d).wait_recv()
-
-        core_arrival(pair).wait_recv()
+            own_arrival().wait_recv()
+            prm_core_arrival(block).wait_recv()
 
         def one(index, inner):
             forward(2 * pair + index)
+
+            @pl.when(foreign & (k < 2) & (index == 0))
+            def _():
+                act_f(k + 1)
+
+            @pl.when(foreign & (k < 2) & (index == 1))
+            def _():
+                act_g(k + 1)
+
+            @pl.when(foreign & (k < 1) & (index == 1))
+            def _():
+                act_e(k + 2)
+
             return inner
 
         return lax.fori_loop(0, 2, one, carry)
@@ -447,6 +621,7 @@
         return ((norm_acc[phase, 0] + norm_acc[phase, 1]) + norm_acc[phase, 2]) + norm_acc[phase, 3]
 
     norm_start(0, norm_value)
+    gather_sent()
 
     for half in (0, 1):
         mine = along[half][0]
@@ -488,42 +663,33 @@
         g3_arrival(d).wait_recv()
     for d in (1, 2, 3):
         total = total + third_in[(pz + d) % 4].astype(F32)
-    spatial_out[0] = total[0:36]
-    temporal_out[0] = total[36:48]
-    norm_out[0] = norm_finish(2)[0:2]
-
-    for d in range(1, 8):
-        prm_copy(d).wait_send()
+    packed_out[0:48] = total
+    packed_out[48:56] = norm_finish(2)
+
     for d in (1, 3, 2):
         for half in (0, 1):
-            z_copy(d, half).wait_send()
             g1_copy(half, d).wait_send()
             g2_copy(half, d).wait_send()
         g3_copy(d).wait_send()
         for phase in range(3):
             n_copy(phase, d).wait_send()
-    for k in range(3):
-        for half in (0, 1):
-            for d in (1, 3, 2):
-                mid_copy(k, half, d).wait_send()
-                last_copy(k, half, d).wait_send()
-    for pair in range(4):
-        core_copy(pair).wait_send()
+
+
+def unpack(packed, spatial_out, temporal_out, norm_out):
+    spatial_out[...] = packed[0:36].reshape(36, 1, CH)
+    temporal_out[...] = packed[36:48].reshape(12, 1, CH)
+    norm_out[0] = packed[48:50]
 
 
 def shards(latents, cotangent, spatial_weight, temporal_weight, norm_gain, norm_shift):
     vmem = pl.BlockSpec(memory_space=pltpu.VMEM)
     anywhere = pl.BlockSpec(memory_space=pl.ANY)
     dma = pltpu.SemaphoreType.DMA
-    return pl.pallas_call(
+    packed = pl.pallas_call(
         kernel,
-        out_shape=(
-            jax.ShapeDtypeStruct((1, 36, CH), F32),
-            jax.ShapeDtypeStruct((1, 12, CH), F32),
-            jax.ShapeDtypeStruct((1, 2, CH), F32),
-        ),
+        out_shape=jax.ShapeDtypeStruct((56, CH), F32),
         in_specs=[vmem, vmem, vmem, vmem, anywhere, anywhere],
-        out_specs=(vmem, vmem, vmem),
+        out_specs=vmem,
         scratch_shapes=[
             pltpu.VMEM((8, WEIGHT_ROWS, CH), BF16),
             pltpu.VMEM((8, 8, CH), F32),
@@ -545,11 +711,15 @@
             pltpu.VMEM((4, 48, CH), BF16),
             pltpu.VMEM((3, 4, 8, CH), F32),
             dma((2,)),
-            dma((4, 2)), dma((3, 2)),
+            dma((1,)), dma((1,)),
+            dma((2, 2)), dma((3, 2)), dma((2,)),
             dma((3, 2, 4)), dma((3, 2, 4)),
             dma((3, 2, 4)), dma((3, 2, 4)),
+            dma((3, 2, 2, 4)), dma((3, 2, 2, 4)),
+            dma((3, 2, 4)), dma((3, 2, 4)),
+            dma((3, 2, 4)), dma((3, 2, 4)),
+            dma((3,)), dma((3,)),
             dma((4,)), dma((4,)),
-            dma((8,)), dma((8,)),
             dma((2, 4)), dma((2, 4)),
             dma((2, 4)), dma((2, 4)),
             dma((4,)), dma((4,)),
@@ -565,6 +735,17 @@
         latents.reshape(CELLS, CH), cotangent.reshape(CELLS, CH), norm_gain, norm_shift,
         spatial_weight, temporal_weight,
     )
+    spatial, temporal, norm = pl.pallas_call(
+        unpack,
+        out_shape=(
+            jax.ShapeDtypeStruct((36, 1, CH), F32),
+            jax.ShapeDtypeStruct((12, 1, CH), F32),
+            jax.ShapeDtypeStruct((1, 2, CH), F32),
+        ),
+        in_specs=[vmem],
+        out_specs=(vmem, vmem, vmem),
+    )(packed)
+    return (spatial.transpose(1, 0, 2), temporal.transpose(1, 0, 2), norm)
 
 
 def solution(mesh):

time: 118 us -> 98.3 us (0.83)
  the two profiles are of different devices: /device:TPU:129 before, /device:TPU:6 now
where the time goes in v2:
time: 98.3 us; the launch traced here: 97.4 us
  Pallas kernels  96.8 us (98%)
    pallas_call x1, Pallas kernels, shards(): pl.pallas_call(kernel, out_shape=jax.ShapeDtypeStruct((56, CH), F32), in_...  95.3 us

profile of v2, /device:TPU:6, one launch (start us, length us, event | category | flops | bytes accessed | tf_op | source)
XLA Modules:
  0.0 97.4 jit_solution(14351434672680530154)
XLA Ops:
  0.6 95.3 %shard_map.85.packed = f32[56,256]{1,0:T(8,128)} custom-call(bf16[256,256]{1,0:T(8,128)(2,1)} %bitcast.4, bf16[256,256]{1,0:T(8,128)(2,1)} %bitcast.5, f32[1,256]{1,0:T(1,128)} %gain_ref.1, f32[1,256]{1,0:T(1,128)} %shift_ref.1, bf16[1,2304,256]{2,1,0:T(8,128)(2,1)} %spatial_ref.1, bf16[1,768,256]{2,1,0:T(8,128)(2,1)} %temporal_ref.1), custom_call_target="tpu_custom_call" | custom-call | flops 6845104128 | bytes 4194304 | tf_op jit(solution)/shard_map/pallas_call | solution.py:688
  96.0 1.5 %shard_map.86 = (f32[36,1,256]{2,1,0:T(1,128)}, f32[12,1,256]{2,1,0:T(1,128)}, f32[1,2,256]{2,1,0:T(2,128)}) custom-call(f32[56,256]{1,0:T(8,128)} %shard_map.85.packed), custom_call_target="tpu_custom_call" | custom-call | tf_op jit(solution)/shard_map/pallas_call | solution.py:738

commit v3 on v2

--- a/solution.py
+++ b/solution.py
@@ -17,24 +17,50 @@
 SLICE = WEIGHT_ROWS // 16
 LONG = WEIGHT_ROWS // 4
 BIT = SLICE // 4
+SUB = SLICE // 2
 SPATIAL_OFFSETS = tuple((dy, dx) for dy in (-1, 0, 1) for dx in (-1, 0, 1))
 TEMPORAL_OFFSETS = (-1, 0, 1)
 F32 = jnp.float32
 BF16 = jnp.bfloat16
 
 
-def group_mean(value):
-    lane = lax.broadcasted_iota(jnp.int32, value.shape, 1)
-    for step in (1, 2, 4):
-        after = pltpu.roll(value, CH - step, axis=1)
-        before = pltpu.roll(value, step, axis=1)
-        value = value + jnp.where((lane & step) == 0, after, before)
-    return value * 0.125
-
-
-def over_groups(row_sum):
-    wide = jnp.broadcast_to(row_sum * (1.0 / CELLS), (8, CH))
-    return group_mean(wide)[0:1]
+def group_values(first, second):
+    rest = jnp.zeros((4, HALF), F32)
+    rows = [first[:, :HALF], first[:, HALF:], second[:, :HALF], second[:, HALF:], rest]
+    value = jnp.concatenate(rows, axis=0)
+    place = lax.broadcasted_iota(jnp.int32, value.shape, 1) % 8
+    values = [value]
+    for step in range(1, 8):
+        ahead = pltpu.roll(value, HALF - step, axis=1)
+        back = pltpu.roll(value, 8 - step, axis=1)
+        values.append(jnp.where(place < 8 - step, ahead, back))
+    return values
+
+
+def added(values):
+    while len(values) > 1:
+        values = [a + b for a, b in zip(values[::2], values[1::2])]
+    return values[0]
+
+
+def widened(rows):
+    return jnp.concatenate([rows[0:1], rows[1:2]], axis=1)
+
+
+def group_statistics(inputs):
+    column = jnp.sum(inputs, axis=0, keepdims=True) * (1.0 / CELLS)
+    within = inputs - column
+    spread = jnp.sum(within * within, axis=0, keepdims=True) * (1.0 / CELLS)
+    values = group_values(column, spread)
+    mean = added(values) * 0.125
+    between = added([(value - mean) * (value - mean) for value in values]) * 0.125
+    scaling = lax.rsqrt(mean[2:4] + between[0:2] + EPSILON)
+    return widened(mean[0:2]), widened(scaling)
+
+
+def group_means(first, second):
+    mean = added(group_values(first, second)) * (0.125 / CELLS)
+    return widened(mean[0:2]), widened(mean[2:4])
 
 
 def shift_x(value, dx):
@@ -370,17 +396,19 @@
         act_a((block + 2) % 4, None)
         pl.when(far_first)(lambda: act_b(0))
         act_b(1)
+        act_b(2)
         act_c(0)
+        act_c(1)
         act_d(0)
-        act_c(1)
+        act_c(2)
+        act_d(1)
         act_e(0)
-        act_b(2)
-        act_d(1)
+        act_d(2)
+        act_e(1)
         act_f(0)
-        act_c(2)
         act_g(0)
-        act_e(1)
-        act_d(2)
+        act_e(2)
+        act_f(1)
 
     def gather_sent():
         def one(k, carry):
@@ -413,11 +441,8 @@
         decoder = s >= 4
         skip = jnp.where(decoder, 1.0, 0.0)
         inputs = hist[s].astype(F32) + skip * hist[jnp.where(decoder, 8 - s, 0)].astype(F32)
-        center = over_groups(jnp.sum(inputs, axis=0, keepdims=True))
-        deviation = inputs - center
-        variance = over_groups(jnp.sum(deviation * deviation, axis=0, keepdims=True))
-        scaling = lax.rsqrt(variance + EPSILON)
-        normed = deviation * scaling
+        center, scaling = group_statistics(inputs)
+        normed = (inputs - center) * scaling
         before = normed * gain + shift
         sigma = jax.nn.sigmoid(before)
         normed_s[s] = normed
@@ -459,17 +484,14 @@
         def one(index, inner):
             forward(2 * pair + index)
 
-            @pl.when(foreign & (k < 2) & (index == 0))
+            @pl.when(foreign & (k == 0) & (index == 0))
             def _():
-                act_f(k + 1)
-
-            @pl.when(foreign & (k < 2) & (index == 1))
+                act_g(1)
+                act_f(2)
+
+            @pl.when(foreign & (k == 0) & (index == 1))
             def _():
-                act_g(k + 1)
-
-            @pl.when(foreign & (k < 1) & (index == 1))
-            def _():
-                act_e(k + 2)
+                act_g(2)
 
             return inner
 
@@ -505,8 +527,10 @@
         middle_grad(s, up)
         grad = before_grad(s)
         normed = normed_s[s]
-        inner = over_groups(gain * jnp.sum(grad, axis=0, keepdims=True))
-        project = over_groups(gain * jnp.sum(grad * normed, axis=0, keepdims=True))
+        inner, project = group_means(
+            gain * jnp.sum(grad, axis=0, keepdims=True),
+            gain * jnp.sum(grad * normed, axis=0, keepdims=True),
+        )
         input_grad = scale_s[s][0:1] * (grad * gain - inner - normed * project)
         ghist[s] = (up.astype(F32) + input_grad).astype(BF16)
         return carry
@@ -535,41 +559,29 @@
         tile = jnp.dot(act_t[...], cols[:, tap * CH : (tap + 1) * CH], preferred_element_type=F32)
         store_rows(tile.astype(BF16), tap * CH, 576, 144, 0)
 
-    def own_part(half, index):
+    def own_part(half, index, sub):
+        rows = pl.ds(sub * SUB, SUB)
         if half == 0:
-            return gsend.at[index, :, :, pl.ds(0, HALF)]
-        return gsend.at[:, index, :, pl.ds(HALF, HALF)]
-
-    def g1_copy(half, d):
+            return gsend.at[index, :, rows, pl.ds(0, HALF)]
+        return gsend.at[:, index, rows, pl.ds(HALF, HALF)]
+
+    def g1_copy(half, sub, d, arrival=False):
         mine, place = along[half]
-        target = (mine + d) % 4
-        return copy(
-            own_part(half, target), first_in.at[half, mine], g1_send.at[half, d],
-            g1_recv.at[half, mine], place(target),
-        )
-
-    def g1_arrival(half, d):
-        mine, place = along[half]
-        source = (mine + d) % 4
-        return copy(
-            own_part(half, source), first_in.at[half, source], g1_send.at[half, d],
-            g1_recv.at[half, source], place(source),
-        )
-
-    def g2_copy(half, d):
+        other = (mine + d) % 4
+        source = other if arrival else mine
+        return copy(
+            own_part(half, other, sub), first_in.at[half, source, :, pl.ds(sub * SUB, SUB)],
+            g1_send.at[half, sub, d], g1_recv.at[half, sub, source], place(other),
+        )
+
+    def g2_copy(half, sub, d, arrival=False):
         mine, place = along[1 - half]
-        target = (mine + d) % 4
-        return copy(
-            first_sum.at[half, target], second_in.at[half, mine], g2_send.at[half, d],
-            g2_recv.at[half, mine], place(target),
-        )
-
-    def g2_arrival(half, d):
-        mine, place = along[1 - half]
-        source = (mine + d) % 4
-        return copy(
-            first_sum.at[half, source], second_in.at[half, source], g2_send.at[half, d],
-            g2_recv.at[half, source], place(source),
+        other = (mine + d) % 4
+        source = other if arrival else mine
+        rows = pl.ds(sub * SUB, SUB)
+        return copy(
+            first_sum.at[half, other, rows], second_in.at[half, source, rows],
+            g2_send.at[half, sub, d], g2_recv.at[half, sub, source], place(other),
         )
 
     def g3_copy(d):
@@ -584,9 +596,10 @@
             third_out.at[source], third_in.at[source], g3_send.at[d], g3_recv.at[source], at_z(source)
         )
 
-    for half in (0, 1):
-        for d in (1, 3, 2):
-            g1_copy(half, d).start()
+    for sub in (0, 1):
+        for half in (0, 1):
+            for d in (1, 3, 2):
+                g1_copy(half, sub, d).start()
 
     axes = along + ((pz, at_z),)
 
@@ -623,27 +636,30 @@
     norm_start(0, norm_value)
     gather_sent()
 
-    for half in (0, 1):
-        mine = along[half][0]
-        for d in (1, 3, 2):
-            g1_arrival(half, d).wait_recv()
-        for index in range(4):
-            if half == 0:
-                total = gsend[mine, index, :, 0:HALF].astype(F32)
-            else:
-                total = gsend[index, mine, :, HALF:CH].astype(F32)
-            for d in (1, 2, 3):
-                total = total + first_in[half, (mine + d) % 4, index].astype(F32)
-            first_sum[half, index] = total.astype(BF16)
-        for d in (1, 3, 2):
-            g2_copy(half, d).start()
+    for sub in (0, 1):
+        for half in (0, 1):
+            mine = along[half][0]
+            rows = slice(sub * SUB, (sub + 1) * SUB)
+            for d in (1, 3, 2):
+                g1_copy(half, sub, d, True).wait_recv()
+            for index in range(4):
+                if half == 0:
+                    total = gsend[mine, index, rows, 0:HALF].astype(F32)
+                else:
+                    total = gsend[index, mine, rows, HALF:CH].astype(F32)
+                for d in (1, 2, 3):
+                    total = total + first_in[half, (mine + d) % 4, index, rows].astype(F32)
+                first_sum[half, index, rows] = total.astype(BF16)
+            for d in (1, 3, 2):
+                g2_copy(half, sub, d).start()
 
     norm_start(1, norm_finish(0))
 
     for half in (0, 1):
         mine = along[1 - half][0]
-        for d in (1, 3, 2):
-            g2_arrival(half, d).wait_recv()
+        for sub in (0, 1):
+            for d in (1, 3, 2):
+                g2_copy(half, sub, d, True).wait_recv()
         total = first_sum[half, mine].astype(F32)
         for d in (1, 2, 3):
             total = total + second_in[half, (mine + d) % 4].astype(F32)
@@ -668,8 +684,9 @@
 
     for d in (1, 3, 2):
         for half in (0, 1):
-            g1_copy(half, d).wait_send()
-            g2_copy(half, d).wait_send()
+            for sub in (0, 1):
+                g1_copy(half, sub, d).wait_send()
+                g2_copy(half, sub, d).wait_send()
         g3_copy(d).wait_send()
         for phase in range(3):
             n_copy(phase, d).wait_send()
@@ -720,8 +737,8 @@
             dma((3, 2, 4)), dma((3, 2, 4)),
             dma((3,)), dma((3,)),
             dma((4,)), dma((4,)),
-            dma((2, 4)), dma((2, 4)),
-            dma((2, 4)), dma((2, 4)),
+            dma((2, 2, 4)), dma((2, 2, 4)),
+            dma((2, 2, 4)), dma((2, 2, 4)),
             dma((4,)), dma((4,)),
             dma((3, 4)), dma((3, 4)),
         ],

time: 98.3 us -> 93.3 us (0.949)
  Pallas kernels: 96.8 us -> 92.4 us
    pallas_call x1, Pallas kernels: 95.3 us -> 90.9 us  [shards(): pl.pallas_call(kernel, out_shape=jax.ShapeDtypeStruct((56, CH), F32), in_...]
where the time goes in v3:
time: 93.3 us; the launch traced here: 93 us
  Pallas kernels  92.4 us (99%)
    pallas_call x1, Pallas kernels, shards(): pl.pallas_call(kernel, out_shape=jax.ShapeDtypeStruct((56, CH), F32), in_...  90.9 us

profile of v3, /device:TPU:6, one launch (start us, length us, event | category | flops | bytes accessed | tf_op | source)
XLA Modules:
  0.0 93.0 jit_solution(12160763971457041817)
XLA Ops:
  0.6 90.9 %shard_map.85.packed = f32[56,256]{1,0:T(8,128)} custom-call(bf16[256,256]{1,0:T(8,128)(2,1)} %bitcast.4, bf16[256,256]{1,0:T(8,128)(2,1)} %bitcast.5, f32[1,256]{1,0:T(1,128)} %gain_ref.1, f32[1,256]{1,0:T(1,128)} %shift_ref.1, bf16[1,2304,256]{2,1,0:T(8,128)(2,1)} %spatial_ref.1, bf16[1,768,256]{2,1,0:T(8,128)(2,1)} %temporal_ref.1), custom_call_target="tpu_custom_call" | custom-call | flops 6845104128 | bytes 4194304 | tf_op jit(solution)/shard_map/pallas_call | solution.py:705
  91.5 1.5 %shard_map.86 = (f32[36,1,256]{2,1,0:T(1,128)}, f32[12,1,256]{2,1,0:T(1,128)}, f32[1,2,256]{2,1,0:T(2,128)}) custom-call(f32[56,256]{1,0:T(8,128)} %shard_map.85.packed), custom_call_target="tpu_custom_call" | custom-call | tf_op jit(solution)/shard_map/pallas_call | solution.py:755

commit v4 on v3

--- a/solution.py
+++ b/solution.py
@@ -17,7 +17,7 @@
 SLICE = WEIGHT_ROWS // 16
 LONG = WEIGHT_ROWS // 4
 BIT = SLICE // 4
-SUB = SLICE // 2
+PARTS = ((144, 48), (0, 96), (96, 48))
 SPATIAL_OFFSETS = tuple((dy, dx) for dy in (-1, 0, 1) for dx in (-1, 0, 1))
 TEMPORAL_OFFSETS = (-1, 0, 1)
 F32 = jnp.float32
@@ -149,15 +149,6 @@
 
     along = ((px, at_x), (py, at_y))
 
-    loads = [
-        pltpu.make_async_copy(spatial_ref.at[0], wall.at[pos, pl.ds(0, SPATIAL)], local_sem.at[0]),
-        pltpu.make_async_copy(
-            temporal_ref.at[0], wall.at[pos, pl.ds(SPATIAL, WEIGHT_ROWS - SPATIAL)], local_sem.at[1]
-        ),
-    ]
-    for load in loads:
-        load.start()
-
     barrier = pltpu.get_barrier_semaphore()
     for d in (1, 2, 3):
         for mine, place in along + ((pz, at_z),):
@@ -169,10 +160,18 @@
             barrier, inc=1, device_id=at_section(other % 8), device_id_type=MESH
         )
 
+    loads = [
+        pltpu.make_async_copy(spatial_ref.at[0], wall.at[pos, pl.ds(0, SPATIAL)], local_sem.at[0]),
+        pltpu.make_async_copy(
+            temporal_ref.at[0], wall.at[pos, pl.ds(SPATIAL, WEIGHT_ROWS - SPATIAL)], local_sem.at[1]
+        ),
+        pltpu.make_async_copy(latents, hist.at[0], local_sem.at[2]),
+        pltpu.make_async_copy(cotangent, ghist.at[8], local_sem.at[3]),
+    ]
+    for load in loads:
+        load.start()
     rest = jnp.zeros((6, CH), F32)
     prm[pos] = jnp.concatenate([gain_ref[...], shift_ref[...], rest], axis=0)
-    hist[0] = latents[...]
-    ghist[8] = cotangent[...]
     for load in loads:
         load.wait()
     pl.semaphore_wait(barrier, 12)
@@ -310,12 +309,17 @@
             ref, ref, core_send.at[k, half, index], core_recv.at[k, half, index], other_core
         )
 
+    def relay_first():
+        z_arrival(order(behind, block), 0).wait_recv()
+        relay_copy(0).start()
+        z_arrival(order(after, block), 1).wait_recv()
+        relay_copy(1).start()
+
     def act_a(pair, relay):
         k = order(pair, block)
         for half in (0, 1):
-            z_arrival(k, half).wait_recv()
-            if relay == half:
-                relay_copy(half).start()
+            if relay != half:
+                z_arrival(k, half).wait_recv()
             for d in (1, 3, 2):
                 line_copy(k, half, d).start()
         prm_arrival(k).wait_recv()
@@ -389,14 +393,15 @@
     own_copy().start()
 
     def gather_start():
+        relay_first()
         act_a(behind, 0)
         act_a(after, 1)
-        far_first = block == 2
-        pl.when(jnp.logical_not(far_first))(lambda: act_b(0))
+        low = jnp.where(block == 2, 1, 0)
+        high = jnp.where(block == 1, 1, 2)
+        act_b(low)
+        act_b(high)
         act_a((block + 2) % 4, None)
-        pl.when(far_first)(lambda: act_b(0))
-        act_b(1)
-        act_b(2)
+        act_b(3 - low - high)
         act_c(0)
         act_c(1)
         act_d(0)
@@ -505,8 +510,7 @@
         other = ghist[jnp.where(encoder, 7 - s, 8)].astype(F32)
         return (ghist[s + 1].astype(F32) + extra * other).astype(BF16)
 
-    def middle_grad(s, up):
-        fill_temporal(tcols, up, -1)
+    def middle_grad(s):
         total = jnp.zeros((CELLS, CH), F32)
         for tap in range(3):
             weight = wall[s, SPATIAL + tap * CH : SPATIAL + (tap + 1) * CH]
@@ -524,7 +528,8 @@
         s = 7 - i
         gain = prm[s][0:1]
         up = upstream(s)
-        middle_grad(s, up)
+        fill_temporal(tcols, up, -1)
+        middle_grad(s)
         grad = before_grad(s)
         normed = normed_s[s]
         inner, project = group_means(
@@ -550,17 +555,8 @@
             ]
             row = stop
 
-    up = upstream(pos)
-    middle_grad(pos, up)
-    for tap in range(3):
-        tile = jnp.dot(mid_t[...], tcols[:, tap * CH : (tap + 1) * CH], preferred_element_type=F32)
-        store_rows(tile.astype(BF16), tap * CH, 192, 48, 144)
-    for tap in range(9):
-        tile = jnp.dot(act_t[...], cols[:, tap * CH : (tap + 1) * CH], preferred_element_type=F32)
-        store_rows(tile.astype(BF16), tap * CH, 576, 144, 0)
-
     def own_part(half, index, sub):
-        rows = pl.ds(sub * SUB, SUB)
+        rows = pl.ds(*PARTS[sub])
         if half == 0:
             return gsend.at[index, :, rows, pl.ds(0, HALF)]
         return gsend.at[:, index, rows, pl.ds(HALF, HALF)]
@@ -570,15 +566,30 @@
         other = (mine + d) % 4
         source = other if arrival else mine
         return copy(
-            own_part(half, other, sub), first_in.at[half, source, :, pl.ds(sub * SUB, SUB)],
+            own_part(half, other, sub), first_in.at[half, source, :, pl.ds(*PARTS[sub])],
             g1_send.at[half, sub, d], g1_recv.at[half, sub, source], place(other),
         )
+
+    def g1_start(sub):
+        for half in (0, 1):
+            for d in (1, 3, 2):
+                g1_copy(half, sub, d).start()
+
+    fill_temporal(tcols, upstream(pos), -1)
+    for tap in range(3):
+        tile = jnp.dot(mid_t[...], tcols[:, tap * CH : (tap + 1) * CH], preferred_element_type=F32)
+        store_rows(tile.astype(BF16), tap * CH, 192, 48, 144)
+    g1_start(0)
+    middle_grad(pos)
+    for tap in range(9):
+        tile = jnp.dot(act_t[...], cols[:, tap * CH : (tap + 1) * CH], preferred_element_type=F32)
+        store_rows(tile.astype(BF16), tap * CH, 576, 144, 0)
 
     def g2_copy(half, sub, d, arrival=False):
         mine, place = along[1 - half]
         other = (mine + d) % 4
         source = other if arrival else mine
-        rows = pl.ds(sub * SUB, SUB)
+        rows = pl.ds(*PARTS[sub])
         return copy(
             first_sum.at[half, other, rows], second_in.at[half, source, rows],
             g2_send.at[half, sub, d], g2_recv.at[half, sub, source], place(other),
@@ -596,10 +607,8 @@
             third_out.at[source], third_in.at[source], g3_send.at[d], g3_recv.at[source], at_z(source)
         )
 
-    for sub in (0, 1):
-        for half in (0, 1):
-            for d in (1, 3, 2):
-                g1_copy(half, sub, d).start()
+    g1_start(1)
+    g1_start(2)
 
     axes = along + ((pz, at_z),)
 
@@ -636,10 +645,10 @@
     norm_start(0, norm_value)
     gather_sent()
 
-    for sub in (0, 1):
+    for sub in (0, 1, 2):
         for half in (0, 1):
             mine = along[half][0]
-            rows = slice(sub * SUB, (sub + 1) * SUB)
+            rows = slice(PARTS[sub][0], sum(PARTS[sub]))
             for d in (1, 3, 2):
                 g1_copy(half, sub, d, True).wait_recv()
             for index in range(4):
@@ -657,7 +666,7 @@
 
     for half in (0, 1):
         mine = along[1 - half][0]
-        for sub in (0, 1):
+        for sub in (0, 1, 2):
             for d in (1, 3, 2):
                 g2_copy(half, sub, d, True).wait_recv()
         total = first_sum[half, mine].astype(F32)
@@ -684,7 +693,7 @@
 
     for d in (1, 3, 2):
         for half in (0, 1):
-            for sub in (0, 1):
+            for sub in (0, 1, 2):
                 g1_copy(half, sub, d).wait_send()
                 g2_copy(half, sub, d).wait_send()
         g3_copy(d).wait_send()
@@ -705,7 +714,7 @@
     packed = pl.pallas_call(
         kernel,
         out_shape=jax.ShapeDtypeStruct((56, CH), F32),
-        in_specs=[vmem, vmem, vmem, vmem, anywhere, anywhere],
+        in_specs=[anywhere, anywhere, vmem, vmem, anywhere, anywhere],
         out_specs=vmem,
         scratch_shapes=[
             pltpu.VMEM((8, WEIGHT_ROWS, CH), BF16),
@@ -727,7 +736,7 @@
             pltpu.VMEM((4, 48, CH), BF16),
             pltpu.VMEM((4, 48, CH), BF16),
             pltpu.VMEM((3, 4, 8, CH), F32),
-            dma((2,)),
+            dma((4,)),
             dma((1,)), dma((1,)),
             dma((2, 2)), dma((3, 2)), dma((2,)),
             dma((3, 2, 4)), dma((3, 2, 4)),
@@ -737,8 +746,8 @@
             dma((3, 2, 4)), dma((3, 2, 4)),
             dma((3,)), dma((3,)),
             dma((4,)), dma((4,)),
-            dma((2, 2, 4)), dma((2, 2, 4)),
-            dma((2, 2, 4)), dma((2, 2, 4)),
+            dma((2, 3, 4)), dma((2, 3, 4)),
+            dma((2, 3, 4)), dma((2, 3, 4)),
             dma((4,)), dma((4,)),
             dma((3, 4)), dma((3, 4)),
         ],

time: 93.3 us -> 90.8 us (0.973)
  Pallas kernels: 92.4 us -> 89.9 us
    pallas_call x1, Pallas kernels: 90.9 us -> 88.4 us  [shards(): pl.pallas_call(kernel, out_shape=jax.ShapeDtypeStruct((56, CH), F32), in_...]
where the time goes in v4:
time: 90.8 us; the launch traced here: 90.5 us
  Pallas kernels  89.9 us (99%)
    pallas_call x1, Pallas kernels, shards(): pl.pallas_call(kernel, out_shape=jax.ShapeDtypeStruct((56, CH), F32), in_...  88.4 us

profile of v4, /device:TPU:6, one launch (start us, length us, event | category | flops | bytes accessed | tf_op | source)
XLA Modules:
  0.0 90.5 jit_solution(3974023528878598453)
XLA Ops:
  0.6 88.4 %shard_map.85.packed = f32[56,256]{1,0:T(8,128)} custom-call(bf16[256,256]{1,0:T(8,128)(2,1)} %bitcast.4, bf16[256,256]{1,0:T(8,128)(2,1)} %bitcast.5, f32[1,256]{1,0:T(1,128)} %gain_ref.1, f32[1,256]{1,0:T(1,128)} %shift_ref.1, bf16[1,2304,256]{2,1,0:T(8,128)(2,1)} %spatial_ref.1, bf16[1,768,256]{2,1,0:T(8,128)(2,1)} %temporal_ref.1), custom_call_target="tpu_custom_call" | custom-call | flops 6845104128 | bytes 4194304 | tf_op jit(solution)/shard_map/pallas_call | solution.py:714
  89.1 1.5 %shard_map.86 = (f32[36,1,256]{2,1,0:T(1,128)}, f32[12,1,256]{2,1,0:T(1,128)}, f32[1,2,256]{2,1,0:T(2,128)}) custom-call(f32[56,256]{1,0:T(8,128)} %shard_map.85.packed), custom_call_target="tpu_custom_call" | custom-call | tf_op jit(solution)/shard_map/pallas_call | solution.py:764

commit v5 on v4

--- a/solution.py
+++ b/solution.py
@@ -414,6 +414,7 @@
         act_g(0)
         act_e(2)
         act_f(1)
+        act_f(2)
 
     def gather_sent():
         def one(k, carry):
@@ -492,7 +493,6 @@
             @pl.when(foreign & (k == 0) & (index == 0))
             def _():
                 act_g(1)
-                act_f(2)
 
             @pl.when(foreign & (k == 0) & (index == 1))
             def _():

time: 90.8 us -> 91.1 us (level)
  no operation moved by 1% of the time
where the time goes in v5:
time: 91.1 us; the launch traced here: 90.6 us
  Pallas kernels  90 us (99%)
    pallas_call x1, Pallas kernels, shards(): pl.pallas_call(kernel, out_shape=jax.ShapeDtypeStruct((56, CH), F32), in_...  88.5 us

profile of v5, /device:TPU:6, one launch (start us, length us, event | category | flops | bytes accessed | tf_op | source)
XLA Modules:
  0.0 90.6 jit_solution(8025996260520194793)
XLA Ops:
  0.6 88.5 %shard_map.85.packed = f32[56,256]{1,0:T(8,128)} custom-call(bf16[256,256]{1,0:T(8,128)(2,1)} %bitcast.4, bf16[256,256]{1,0:T(8,128)(2,1)} %bitcast.5, f32[1,256]{1,0:T(1,128)} %gain_ref.1, f32[1,256]{1,0:T(1,128)} %shift_ref.1, bf16[1,2304,256]{2,1,0:T(8,128)(2,1)} %spatial_ref.1, bf16[1,768,256]{2,1,0:T(8,128)(2,1)} %temporal_ref.1), custom_call_target="tpu_custom_call" | custom-call | flops 6845104128 | bytes 4194304 | tf_op jit(solution)/shard_map/pallas_call | solution.py:714
  89.2 1.5 %shard_map.86 = (f32[36,1,256]{2,1,0:T(1,128)}, f32[12,1,256]{2,1,0:T(1,128)}, f32[1,2,256]{2,1,0:T(2,128)}) custom-call(f32[56,256]{1,0:T(8,128)} %shard_map.85.packed), custom_call_target="tpu_custom_call" | custom-call | tf_op jit(solution)/shard_map/pallas_call | solution.py:764
